TPU v7x, 256 devices: a whole 4x4x8 slice. The times are simulated.
256 devices in a mesh: ctx: 64 (over x_hi, y, z), head: 4 (over x_lo, core).
Axes of the slice: x: 4 (x_hi: 2, x_lo: 2; x = x_hi * 2 + x_lo), y: 4, z: 8, core: 2. Of those that a mesh axis runs over, the one named last changes fastest.
Arguments:
- queries: bfloat16 [16384, 6144], P(('ctx', 'head')), may hold values from -42 to 42
- key_head_columns: bfloat16 [16384, 512], P(('ctx', 'head')), may hold values from -4 to 4
- value_head_columns: bfloat16 [16384, 512], P(('ctx', 'head')), may hold values from -6 to 6
- output_gradient: bfloat16 [16384, 6144], P(('ctx', 'head')), may hold values from -6 to 6
- file_starts: int32 [33], replicated, may hold values from 0 to 16320, as said below
- file_imports: int32 [33, 4], replicated, may hold values from -1 to 32, as said below
- header_lens: int32 [33], replicated, may hold values from 16 to 64
Outputs:
- grad_queries: float32 [16384, 6144], P(('ctx', 'head'))
- key_gradient: float32 [16384, 512], P(('ctx', 'head'))
- value_gradient: float32 [16384, 512], P(('ctx', 'head'))
Inputs may be any that keep to these rules, and one draw needn't show every extreme that they name: `file_starts`: Increasing; the first is 0 and the last is 16320; each is a multiple of 64; no two lie in the same aligned block of 256 tokens; each file has 64 tokens or more. `file_imports`: each row lists distinct files other than its own, then -1 in the unused places; file 0 imports nothing.
All inputs are finite; a program needn't handle non-finite values.
Results may differ from a plain program's by a relative error of at most 0.004.
Values may be sent and summed in bfloat16 or wider, within the bound.
A program may use at most 64 MiB of HBM per device.

v0:
```python
import math

import jax
import jax.numpy as jnp
from jax import lax
from jax.sharding import Mesh
from jax.sharding import PartitionSpec as P

WIN = 1024
HDR = 64
HEAD = ("head_0", "head_1")
CTX = ("ctx_0", "ctx_1", "ctx_2")
CTX_HEAD = ("ctx_0", "ctx_1", "ctx_2", "head_0", "head_1")


def in_blocks(array, dim, devices):
    before, after = (array.shape[:dim], array.shape[dim + 1 :])
    return jnp.moveaxis(array.reshape(*before, devices, -1, *after), dim, 0)


def joined_along(parts, dim):
    dims = list(parts.shape[1:])
    dims[dim] *= parts.shape[0]
    return jnp.moveaxis(parts, 0, dim).reshape(dims)


def exchange_in_order(parts, axes, turns):
    dims = [lax.axis_size(a) for a in axes]
    parts = parts.reshape(*dims, *parts.shape[1:])
    for k in turns:
        parts = lax.all_to_all(parts, axes[k], split_axis=k, concat_axis=k, tiled=True)
    return parts.reshape(-1, *parts.shape[len(axes) :])


def two_step_exchange(array, groups, turns, split_dim, concat_dim):
    devices = lax.axis_size(groups[0]) * lax.axis_size(groups[1])
    parts = in_blocks(array, split_dim, devices)
    return joined_along(exchange_in_order(parts, groups, turns), concat_dim)


def passed_along(value, axis, steps):
    count = lax.axis_size(axis)
    first, last = (max(0, -steps), min(count, count - steps))
    return lax.ppermute(value, axis, [(source, source + steps) for source in range(first, last)])


def stacked_from(array, axes, turns):
    parts = array[None]
    for k in turns:
        parts = lax.all_gather(parts, axes[k], axis=0, tiled=True)
    carried = [lax.axis_size(axes[k]) for k in reversed(turns)]
    parts = parts.reshape(*carried, *array.shape)
    turned = sorted(range(len(turns)), key=lambda place: turns[len(turns) - 1 - place])
    return parts.transpose(*turned, *range(len(turns), parts.ndim)).reshape(-1, *array.shape)


def gather_axes(array, axes, turns, dim):
    return joined_along(stacked_from(array, axes, turns), dim)


def own_block(parts, axes, turns):
    inside = parts.shape[1:]
    parts = parts.reshape(*(lax.axis_size(a) for a in axes), *inside)
    parts = jnp.moveaxis(parts, turns, range(len(axes))).reshape(-1, *inside)
    for k in turns:
        parts = lax.psum_scatter(parts, axes[k], scatter_dimension=0, tiled=True)
    return parts[0]


def sum_by_axis(array, axes, turns, dim):
    devices = lax.axis_size(axes)
    return own_block(in_blocks(array, dim, devices), axes, turns)


def local_files(file_starts, file_imports, header_lens, offset_base, span_rows):
    places = offset_base + jnp.arange(span_rows, dtype=jnp.int32)
    before = file_starts[None, :] <= places[:, None]
    file_of = jnp.sum(before.astype(jnp.int32), axis=1) - 1
    file_begin = jnp.max(jnp.where(before, file_starts[None, :], 0), axis=1)
    lower_file = file_of[0]
    upper_file = file_of[span_rows - 1]
    per_file = file_imports.shape[1]
    lower_list = lax.dynamic_slice_in_dim(file_imports, lower_file, 1, 0)[0]
    upper_list = lax.dynamic_slice_in_dim(file_imports, upper_file, 1, 0)[0]
    targets = jnp.concatenate([lower_list, upper_list])
    source_file = jnp.concatenate(
        [jnp.full((per_file,), lower_file, jnp.int32), jnp.full((per_file,), upper_file, jnp.int32)]
    )
    usable = (targets >= 0) & (
        (jnp.arange(2 * per_file, dtype=jnp.int32) < per_file) | (upper_file != lower_file)
    )
    matches = jnp.arange(file_starts.shape[0], dtype=jnp.int32)[None, :] == targets[:, None]
    target_start = jnp.sum(jnp.where(matches, file_starts[None, :], 0), axis=1)
    target_len = jnp.sum(jnp.where(matches, header_lens[None, :], 0), axis=1)
    return (places, file_of, file_begin, source_file, usable, target_start, target_len)


def visibility(places, file_of, file_begin, key_places, source_file, usable, target_len):
    window_ok = (
        (key_places[None, :] <= places[:, None])
        & (key_places[None, :] > places[:, None] - WIN)
        & (key_places[None, :] >= file_begin[:, None])
    )
    offsets = jnp.arange(usable.shape[0] * HDR, dtype=jnp.int32) % HDR
    header_ok = jnp.repeat(usable, HDR) & (offsets < jnp.repeat(target_len, HDR))
    header_vis = header_ok[None, :] & (file_of[:, None] == jnp.repeat(source_file, HDR)[None, :])
    return jnp.concatenate([window_ok, header_vis], axis=1)


def per_device(
    queries,
    key_head_columns,
    value_head_columns,
    output_gradient,
    file_starts,
    file_imports,
    header_lens,
):
    query_rows, key_rows, value_rows, grad_rows = (
        two_step_exchange(queries, ("head_0", "head_1"), (1, 0), 1, 0),
        two_step_exchange(key_head_columns, ("head_0", "head_1"), (1, 0), 1, 0),
        two_step_exchange(value_head_columns, ("head_0", "head_1"), (1, 0), 1, 0),
        two_step_exchange(output_gradient, ("head_0", "head_1"), (1, 0), 1, 0),
    )
    tokens_here = key_rows.shape[0]
    head_size = key_rows.shape[1]
    queries_per_group = query_rows.shape[1] // head_size
    shard_index = lax.axis_index(CTX)
    ctx_count = lax.axis_size(CTX)
    offset_base = shard_index * tokens_here
    scaling = 1.0 / math.sqrt(head_size)
    reach = WIN // tokens_here
    places, file_of, file_begin, source_file, usable, target_start, target_len = local_files(
        file_starts, file_imports, header_lens, offset_base, tokens_here
    )
    block_count = source_file.shape[0]
    stacked = jnp.concatenate([key_rows, value_rows], axis=1)
    earlier = []
    moving = stacked
    for distance in range(1, reach + 1):
        moving = passed_along(moving, CTX, 1)
        earlier.append(moving)
    inside = (file_starts >= offset_base) & (file_starts < offset_base + tokens_here)
    own_offset = jnp.sum(jnp.where(inside, file_starts - offset_base, 0))
    own_header = lax.dynamic_slice_in_dim(stacked, own_offset, HDR, 0)
    all_headers = gather_axes(own_header, CTX, (0, 2, 1), 0)
    header_rows = jnp.concatenate(
        [
            lax.dynamic_slice_in_dim(all_headers, target_start[index] // tokens_here * HDR, HDR, 0)
            for index in range(block_count)
        ],
        axis=0,
    )
    key_table = jnp.concatenate(earlier[::-1] + [stacked, header_rows], axis=0)
    key_matrix = key_table[:, :head_size]
    value_matrix = key_table[:, head_size:]
    window_len = (reach + 1) * tokens_here
    key_places = offset_base - reach * tokens_here + jnp.arange(window_len, dtype=jnp.int32)
    visible = visibility(places, file_of, file_begin, key_places, source_file, usable, target_len)
    heads_block = max(
        (
            divisor
            for divisor in range(1, queries_per_group + 1)
            if queries_per_group % divisor == 0 and divisor * tokens_here <= max(512, tokens_here)
        )
    )
    block_total = queries_per_group // heads_block
    query_blocks = (
        query_rows.reshape(tokens_here, queries_per_group, head_size)
        .transpose(1, 0, 2)
        .reshape(block_total, heads_block, tokens_here, head_size)
    )
    grad_blocks = (
        grad_rows.reshape(tokens_here, queries_per_group, head_size)
        .transpose(1, 0, 2)
        .reshape(block_total, heads_block, tokens_here, head_size)
    )

    def attend(carry, inputs):
        key_gradient_sum, value_gradient_sum = carry
        query_block, grad_block = inputs
        scores = (
            jnp.einsum("htd,kd->htk", query_block, key_matrix, preferred_element_type=jnp.float32)
            * scaling
        )
        scores = jnp.where(visible[None], scores, -jnp.inf)
        ceiling = jnp.max(scores, axis=-1, keepdims=True)
        log_total = ceiling + jnp.log(jnp.sum(jnp.exp(scores - ceiling), axis=-1, keepdims=True))
        weights = jnp.exp(scores - log_total)
        grad_weights = jnp.einsum(
            "htd,kd->htk", grad_block, value_matrix, preferred_element_type=jnp.float32
        )
        centre = jnp.sum(weights * grad_weights, axis=-1, keepdims=True)
        grad_scores = (weights * (grad_weights - centre)).astype(jnp.bfloat16)
        weights_low = weights.astype(jnp.bfloat16)
        grad_query = (
            jnp.einsum("htk,kd->htd", grad_scores, key_matrix, preferred_element_type=jnp.float32)
            * scaling
        )
        key_gradient_sum = (
            key_gradient_sum
            + jnp.einsum(
                "htk,htd->kd", grad_scores, query_block, preferred_element_type=jnp.float32
            )
            * scaling
        )
        value_gradient_sum = value_gradient_sum + jnp.einsum(
            "htk,htd->kd", weights_low, grad_block, preferred_element_type=jnp.float32
        )
        return ((key_gradient_sum, value_gradient_sum), grad_query)

    empty_gradient = jnp.zeros((key_table.shape[0], head_size), jnp.float32)
    (key_gradient_sum, value_gradient_sum), grad_query = lax.scan(
        attend, (empty_gradient, empty_gradient), (query_blocks, grad_blocks)
    )
    grad_query = (
        grad_query.reshape(queries_per_group, tokens_here, head_size)
        .transpose(1, 0, 2)
        .reshape(tokens_here, queries_per_group * head_size)
    )
    combined = jnp.concatenate([key_gradient_sum, value_gradient_sum], axis=1)

    def window_part(index):
        return combined[index * tokens_here : (index + 1) * tokens_here]

    collected = window_part(reach)
    carried = window_part(0)
    for distance in range(1, reach + 1):
        carried = passed_along(carried, CTX, -1)
        if distance < reach:
            carried = carried + window_part(distance)
    collected = collected + carried
    header_part = combined[window_len:]
    slot_table = jnp.zeros((ctx_count * HDR, 2 * head_size), jnp.float32)
    for index in range(block_count):
        at_row = target_start[index] // tokens_here * HDR
        current = lax.dynamic_slice_in_dim(slot_table, at_row, HDR, 0)
        slot_table = lax.dynamic_update_slice_in_dim(
            slot_table, current + header_part[index * HDR : (index + 1) * HDR], at_row, 0
        )
    arriving = sum_by_axis(slot_table, CTX, (1, 2, 0), 0)
    current = lax.dynamic_slice_in_dim(collected, own_offset, HDR, 0)
    collected = lax.dynamic_update_slice_in_dim(collected, current + arriving, own_offset, 0)
    grad_queries, key_gradient, value_gradient = (
        lax.all_to_all(grad_query, HEAD, split_axis=0, concat_axis=1, tiled=True),
        lax.all_to_all(collected[:, :head_size], HEAD, split_axis=0, concat_axis=1, tiled=True),
        lax.all_to_all(collected[:, head_size:], HEAD, split_axis=0, concat_axis=1, tiled=True),
    )
    return (grad_queries, key_gradient, value_gradient)


def solution(mesh):
    split = Mesh(
        mesh.devices.reshape(2, 4, 8, 2, 2), ("ctx_0", "ctx_1", "ctx_2", "head_0", "head_1")
    )
    placed = (
        P(CTX_HEAD, None),
        P(CTX_HEAD, None),
        P(CTX_HEAD, None),
        P(CTX_HEAD, None),
        P(),
        P(),
        P(),
    )
    return jax.shard_map(
        per_device,
        mesh=split,
        in_specs=placed,
        out_specs=(P(CTX_HEAD, None), P(CTX_HEAD, None), P(CTX_HEAD, None)),
        check_vma=False,
    )
```

profile of v0, /device:TPU:1, one launch (start us, length us, event | category | flops | bytes accessed | tf_op | source)
XLA Modules:
  0.0 381.8 jit_solution(10581533873204575703)
XLA Ops:
  8.7 6.5 %all-to-all-start.4 = ((bf16[2,2,64,128]{3,2,0,1:T(8,128)(2,1)}), bf16[2,2,64,128]{3,2,0,1:T(8,128)(2,1)S(1)}, u32[]{:S(2)}, u32[]{:S(2)}) async-start(bf16[2,2,64,128]{3,2,0,1:T(8,128)(2,1)} %copy.125), calls=%async_computation.4 | async-start | bytes 131072 | tf_op jit(solution)/shard_map/all_to_all | solution.py:31
  16.7 3.3 all-to-all-start.2
  21.1 3.3 all-to-all-start.5
  25.0 2.3 all-to-all-done.5
  27.3 3.3 all-to-all-start.3
  30.7 1.3 fusion.41
  34.0 4.9 %all-gather = bf16[128,256]{1,0:T(8,128)(2,1)S(1)} all-gather(bf16[64,256]{1,0:T(8,128)(2,1)S(1)} %fusion.33), channel_id=2, replica_groups=mesh['ctx_0'=2,'ctx_1'=4,'ctx_2'=8,'head_0'=2,'head_1'=2] {'ctx_0'}, dimensions={0}, use_global_device_ids=true | all-gather | bytes 98304 | tf_op jit(solution)/shard_map/all_gather | solution.py:50
  38.9 23.3 %all_gather.10 = bf16[16,64,256]{2,1,0:T(8,128)(2,1)} all-gather(bf16[2,64,256]{2,1,0:T(8,128)(2,1)S(1)} %bitcast.156), channel_id=1, replica_groups=mesh['ctx_0'=2,'ctx_1'=4,'ctx_2'=8,'head_0'=2,'head_1'=2] {'ctx_2'}, dimensions={0}, use_global_device_ids=true | all-gather | bytes 589824 | tf_op jit(solution)/shard_map/all_gather | solution.py:50
  62.2 2.3 reshape.122
  65.6 13.0 %all-to-all-start.6 = ((bf16[2,2,64,1536]{3,2,0,1:T(8,128)(2,1)}), bf16[2,2,64,1536]{3,2,0,1:T(8,128)(2,1)S(1)}, u32[]{:S(2)}, u32[]{:S(2)}) async-start(bf16[2,2,64,1536]{3,2,0,1:T(8,128)(2,1)} %copy.129), calls=%async_computation.6 | async-start | bytes 1572864 | tf_op jit(solution)/shard_map/all_to_all | solution.py:31
  86.2 3.6 all-to-all-start
  91.5 2.6 collective-permute-start
  94.2 3.6 all-to-all-start.7
  121.9 2.6 collective-permute-start.1
  124.6 2.6 collective-permute-done.1
  127.1 4.1 %collective-permute-start.2 = (bf16[256,256]{1,0:T(8,128)(2,1)S(1)}, bf16[256,256]{1,0:T(8,128)(2,1)S(1)}, u32[]{:S(2)}, u32[]{:S(2)}) collective-permute-start(bf16[256,256]{1,0:T(8,128)(2,1)S(1)} %collective-permute-done.1), channel_id=1, source_target_pairs={{0,4},{4,8},{8,12},{12,16},{16,20},{20,24},{24,28},{28,32},{32,36}... | collective-permute-start | bytes 393224 | tf_op jit(solution)/shard_map/ppermute | solution.py:44
  131.2 4.3 %all-to-all-start.1 = ((bf16[2,2,64,1536]{3,2,1,0:T(8,128)(2,1)}), bf16[2,2,64,1536]{3,2,1,0:T(8,128)(2,1)}, u32[]{:S(2)}, u32[]{:S(2)}) async-start(bf16[2,2,64,1536]{3,2,1,0:T(8,128)(2,1)} %copy.119), calls=%async_computation.1 | async-start | bytes 1572864 | tf_op jit(solution)/shard_map/all_to_all | solution.py:31
  135.8 2.8 collective-permute-start.3
  138.6 1.5 reshape_reshape_reshape.7
  140.2 1.4 copy.131
  141.6 3.5 all-to-all-done.1
  145.1 2.4 reshape_reshape_reshape.6
  147.4 2.3 copy.120
  153.1 1.7 copy.127
  160.9 67.9 %while.15 = (s32[]{:T(128)}, f32[1792,128]{1,0:T(8,128)S(1)}, f32[1792,128]{1,0:T(8,128)}, f32[6,2,256,128]{3,2,1,0:T(8,128)}, pred[256,1792]{1,0:T(8,128)(4,1)S...) while((s32[]{:T(128)}, f32[1792,128]{1,0:T(8,128)S(1)}, ...), condition=%wide.region_9.10_spmd.clone, body=%wide.region_5.9_spmd.clone.sunk | while | flops 1188461568 | bytes 80503144 | solution.py:213
  161.0 2.0 fusion.67
  165.6 1.4 fusion.70
  166.9 2.1 fusion.68
  169.0 2.9 fusion.69
  172.0 2.0 fusion.67
  176.6 1.4 fusion.70
  178.0 2.1 fusion.68
  180.1 3.3 fusion.69
  183.4 2.0 fusion.67
  188.0 1.4 fusion.70
  189.3 2.1 fusion.68
  191.5 3.3 fusion.69
  194.8 2.0 fusion.67
  199.4 1.4 fusion.70
  200.7 2.1 fusion.68
  202.8 3.3 fusion.69
  206.1 2.0 fusion.67
  210.7 1.4 fusion.70
  212.1 2.1 fusion.68
  214.2 3.3 fusion.69
  217.5 2.0 fusion.67
  222.1 1.4 fusion.70
  223.5 2.1 fusion.68
  225.6 3.3 fusion.69
  230.7 2.3 copy.134
  233.0 56.0 %reduce-scatter.4.cloned.1.call-done = f32[16,64,256]{2,1,0:T(8,128)} async-done(((f32[64,64,256]{2,1,0:T(8,128)}), f32[16,64,256]{2,1,0:T(8,128)}) %reduce-scatter.4.cloned.1.call-update) | async-done | bytes 1048592 | tf_op jit(solution)/shard_map/reduce_scatter | solution.py:66
  290.4 7.8 %collective-permute-done.4 = f32[256,256]{1,0:T(8,128)S(1)} collective-permute-done((f32[256,256]{1,0:T(8,128)S(1)}, f32[256,256]{1,0:T(8,128)S(1)}, u32[]{:S(2)}, u32[]{:S(2)}) %collective-permute-start.4) | collective-permute-done | bytes 262176 | tf_op jit(solution)/shard_map/ppermute | solution.py:44
  298.3 1.3 collective-permute-start.5
  299.6 8.4 %collective-permute-done.5 = f32[256,256]{1,0:T(8,128)S(1)} collective-permute-done((f32[256,256]{1,0:T(8,128)S(1)}, f32[256,256]{1,0:T(8,128)S(1)}, u32[]{:S(2)}, u32[]{:S(2)}) %collective-permute-start.5) | collective-permute-done | bytes 262176 | tf_op jit(solution)/shard_map/ppermute | solution.py:44
  309.3 2.4 copy.149
  311.7 1.4 all_to_all.74
  313.1 7.4 %all-to-all-start.8 = ((f32[4,64,1536]{2,1,0:T(8,128)}), f32[4,64,1536]{2,1,0:T(8,128)S(1)}, u32[]{:S(2)}, u32[]{:S(2)}) async-start(f32[4,64,1536]{2,1,0:T(8,128)} %all_to_all.74), calls=%async_computation.8 | async-start | bytes 3145728 | tf_op jit(solution)/shard_map/all_to_all | solution.py:245
  322.8 4.6 %reduce-scatter.6.cloned.1.call-done = f32[2,64,256]{2,1,0:T(8,128)} async-done(((f32[16,64,256]{2,1,0:T(8,128)}), f32[2,64,256]{2,1,0:T(8,128)}) %reduce-scatter.6.cloned.1.call-update) | async-done | bytes 131088 | tf_op jit(solution)/shard_map/reduce_scatter | solution.py:66
  327.4 4.0 %collective-permute-done.7 = f32[256,256]{1,0:T(8,128)S(1)} collective-permute-done((f32[256,256]{1,0:T(8,128)S(1)}, f32[256,256]{1,0:T(8,128)S(1)}, u32[]{:S(2)}, u32[]{:S(2)}) %collective-permute-start.7) | collective-permute-done | bytes 262176 | tf_op jit(solution)/shard_map/ppermute | solution.py:44
  332.4 24.7 %reduce-scatter.8.cloned.1.call-done = f32[1,64,256]{2,1,0:T(8,128)} async-done(((f32[2,64,256]{2,1,0:T(8,128)}), f32[1,64,256]{2,1,0:T(8,128)}) %reduce-scatter.8.cloned.1.call-update) | async-done | bytes 65552 | tf_op jit(solution)/shard_map/reduce_scatter | solution.py:66
  359.3 3.8 all-to-all-start.10
  364.3 2.3 all-to-all-done.10
  366.6 4.3 %all-to-all-start.9 = ((f32[4,64,128]{2,1,0:T(8,128)}), f32[4,64,128]{2,1,0:T(8,128)S(1)}, u32[]{:S(2)}, u32[]{:S(2)}) async-start(f32[4,64,128]{2,1,0:T(8,128)} %bitcast.35), calls=%async_computation.12 | async-start | bytes 262144 | tf_op jit(solution)/shard_map/all_to_all | solution.py:246
  371.6 2.9 all-to-all-done.9
  (228 shorter events, 51.2 us)
Async XLA Ops:
  8.7 8.0 %all-to-all-start.4 = ((bf16[2,2,64,128]{3,2,0,1:T(8,128)(2,1)}), bf16[2,2,64,128]{3,2,0,1:T(8,128)(2,1)S(1)}, u32[]{:S(2)}, u32[]{:S(2)}) async-start(bf16[2,2,64,128]{3,2,0,1:T(8,128)(2,1)} %copy.125), calls=%async_computation.4 | async-start | bytes 131072 | tf_op jit(solution)/shard_map/all_to_all | solution.py:31
  16.7 4.4 %all-to-all-start.2 = ((bf16[2,2,64,128]{3,2,0,1:T(8,128)(2,1)}), bf16[2,2,64,128]{3,2,0,1:T(8,128)(2,1)S(1)}, u32[]{:S(2)}, u32[]{:S(2)}) async-start(bf16[2,2,64,128]{3,2,0,1:T(8,128)(2,1)} %copy.122), calls=%async_computation.2 | async-start | bytes 131072 | tf_op jit(solution)/shard_map/all_to_all | solution.py:31
  21.1 6.3 %all-to-all-start.5 = ((bf16[2,2,64,128]{3,2,1,0:T(8,128)(2,1)}), bf16[2,2,64,128]{3,2,1,0:T(8,128)(2,1)S(1)}, u32[]{:S(2)}, u32[]{:S(2)}) async-start(bf16[2,2,64,128]{3,2,1,0:T(8,128)(2,1)} %copy.126), calls=%async_computation.5 | async-start | bytes 131072 | tf_op jit(solution)/shard_map/all_to_all | solution.py:31
  27.3 6.6 %all-to-all-start.3 = ((bf16[2,2,64,128]{3,2,1,0:T(8,128)(2,1)}), bf16[2,2,64,128]{3,2,1,0:T(8,128)(2,1)S(1)}, u32[]{:S(2)}, u32[]{:S(2)}) async-start(bf16[2,2,64,128]{3,2,1,0:T(8,128)(2,1)} %copy.123), calls=%async_computation.3 | async-start | bytes 131072 | tf_op jit(solution)/shard_map/all_to_all | solution.py:31
  30.6 122.4 %all-gather.3.cloned.1.call-start = ((), (), s32[]{:S(2)}) async-start(), calls=%async_computation.14 | async-start | bytes 2621440 | tf_op jit(solution)/shard_map/all_gather | solution.py:50
  38.9 39.8 %copy-start.11 = (s32[33]{0:T(128)S(1)}, s32[33]{0:T(128)}, u32[]{:S(2)}) copy-start(s32[33]{0:T(128)} %param.13) | copy-start | bytes 400
  38.9 44.3 %copy-start.9 = (bf16[64,6144]{1,0:T(8,128)(2,1)S(1)}, bf16[64,6144]{1,0:T(8,128)(2,1)}, u32[]{:S(2)}) copy-start(bf16[64,6144]{1,0:T(8,128)(2,1)} %param.9) | copy-start | bytes 2359300
  65.6 20.6 %all-to-all-start.6 = ((bf16[2,2,64,1536]{3,2,0,1:T(8,128)(2,1)}), bf16[2,2,64,1536]{3,2,0,1:T(8,128)(2,1)S(1)}, u32[]{:S(2)}, u32[]{:S(2)}) async-start(bf16[2,2,64,1536]{3,2,0,1:T(8,128)(2,1)} %copy.129), calls=%async_computation.6 | async-start | bytes 1572864 | tf_op jit(solution)/shard_map/all_to_all | solution.py:31
  83.2 7.5 %copy-start.10 = (s32[33,4]{0,1:T(4,128)S(1)}, s32[33,4]{0,1:T(4,128)}, u32[]{:S(2)}) copy-start(s32[33,4]{0,1:T(4,128)} %param.14) | copy-start | bytes 1588
  83.9 13.8 %copy-start.12 = (s32[33]{0:T(128)S(1)}, s32[33]{0:T(128)}, u32[]{:S(2)}) copy-start(s32[33]{0:T(128)} %param.15) | copy-start | bytes 400
  86.2 8.0 %all-to-all-start = ((bf16[2,2,64,1536]{3,2,0,1:T(8,128)(2,1)}), bf16[2,2,64,1536]{3,2,0,1:T(8,128)(2,1)S(1)}, u32[]{:S(2)}, u32[]{:S(2)}) async-start(bf16[2,2,64,1536]{3,2,0,1:T(8,128)(2,1)} %copy.118), calls=%async_computation | async-start | bytes 1572864 | tf_op jit(solution)/shard_map/all_to_all | solution.py:31
  91.5 30.4 %collective-permute-start = (bf16[256,256]{1,0:T(8,128)(2,1)S(1)}, bf16[256,256]{1,0:T(8,128)(2,1)S(1)}, u32[]{:S(2)}, u32[]{:S(2)}) collective-permute-start(bf16[256,256]{1,0:T(8,128)(2,1)S(1)} %pad_maximum_fusion), channel_id=1, source_target_pairs={{0,4},{4,8},{8,12},{12,16},{16,20},{20,24},{24,28},{28,32},{32,36}... | collective-permute-start | bytes 393224 | tf_op jit(solution)/shard_map/ppermute | solution.py:44
  94.2 37.1 %all-to-all-start.7 = ((bf16[2,2,64,1536]{3,2,1,0:T(8,128)(2,1)}), bf16[2,2,64,1536]{3,2,1,0:T(8,128)(2,1)S(1)}, u32[]{:S(2)}, u32[]{:S(2)}) async-start(bf16[2,2,64,1536]{3,2,1,0:T(8,128)(2,1)} %copy.130), calls=%async_computation.7 | async-start | bytes 1572864 | tf_op jit(solution)/shard_map/all_to_all | solution.py:31
  121.9 5.2 %collective-permute-start.1 = (bf16[256,256]{1,0:T(8,128)(2,1)S(1)}, bf16[256,256]{1,0:T(8,128)(2,1)S(1)}, u32[]{:S(2)}, u32[]{:S(2)}) collective-permute-start(bf16[256,256]{1,0:T(8,128)(2,1)S(1)} %collective-permute-done), channel_id=1, source_target_pairs={{0,4},{4,8},{8,12},{12,16},{16,20},{20,24},{24,28},{28,32},{32,36}... | collective-permute-start | bytes 393224 | tf_op jit(solution)/shard_map/ppermute | solution.py:44
  127.1 8.7 %collective-permute-start.2 = (bf16[256,256]{1,0:T(8,128)(2,1)S(1)}, bf16[256,256]{1,0:T(8,128)(2,1)S(1)}, u32[]{:S(2)}, u32[]{:S(2)}) collective-permute-start(bf16[256,256]{1,0:T(8,128)(2,1)S(1)} %collective-permute-done.1), channel_id=1, source_target_pairs={{0,4},{4,8},{8,12},{12,16},{16,20},{20,24},{24,28},{28,32},{32,36}... | collective-permute-start | bytes 393224 | tf_op jit(solution)/shard_map/ppermute | solution.py:44
  131.2 13.8 %all-to-all-start.1 = ((bf16[2,2,64,1536]{3,2,1,0:T(8,128)(2,1)}), bf16[2,2,64,1536]{3,2,1,0:T(8,128)(2,1)}, u32[]{:S(2)}, u32[]{:S(2)}) async-start(bf16[2,2,64,1536]{3,2,1,0:T(8,128)(2,1)} %copy.119), calls=%async_computation.1 | async-start | bytes 1572864 | tf_op jit(solution)/shard_map/all_to_all | solution.py:31
  135.5 153.5 %reduce-scatter.4.cloned.1.call-start = ((), (), s32[]{:S(2)}) async-start(), calls=%async_computation.15 | async-start | bytes 5242880 | tf_op jit(solution)/shard_map/reduce_scatter | solution.py:66
  135.8 14.0 %collective-permute-start.3 = (bf16[256,256]{1,0:T(8,128)(2,1)S(1)}, bf16[256,256]{1,0:T(8,128)(2,1)S(1)}, u32[]{:S(2)}, u32[]{:S(2)}) collective-permute-start(bf16[256,256]{1,0:T(8,128)(2,1)S(1)} %collective-permute-done.2), channel_id=1, source_target_pairs={{0,4},{4,8},{8,12},{12,16},{16,20},{20,24},{24,28},{28,32},{32,36}... | collective-permute-start | bytes 393224 | tf_op jit(solution)/shard_map/ppermute | solution.py:44
  160.9 2.7 copy-start.2
  161.0 2.7 copy-start.4
  161.0 3.6 copy-start.6
  169.0 3.0 copy-start.3
  169.0 3.0 copy-start.5
  169.0 3.0 copy-start.7
  172.0 2.7 copy-start.2
  172.0 2.7 copy-start.4
  172.0 3.6 copy-start.6
  180.0 3.3 copy-start.3
  180.1 3.3 copy-start.5
  180.1 3.3 copy-start.7
  183.4 2.7 copy-start.2
  183.4 2.7 copy-start.4
  183.4 3.6 copy-start.6
  191.4 3.3 copy-start.3
  191.4 3.3 copy-start.5
  191.4 3.3 copy-start.7
  194.7 2.7 copy-start.2
  194.7 2.7 copy-start.4
  194.8 3.6 copy-start.6
  202.8 3.3 copy-start.3
  202.8 3.3 copy-start.5
  202.8 3.3 copy-start.7
  206.1 2.7 copy-start.2
  206.1 2.7 copy-start.4
  206.1 3.6 copy-start.6
  214.2 3.3 copy-start.3
  214.2 3.3 copy-start.5
  214.2 3.3 copy-start.7
  217.5 2.7 copy-start.2
  217.5 2.7 copy-start.4
  217.5 3.6 copy-start.6
  225.5 3.3 copy-start.3
  225.6 3.3 copy-start.5
  225.6 3.3 copy-start.7
  230.2 77.8 %copy-start.8 = (f32[1792,256]{1,0:T(8,128)}, f32[1792,256]{1,0:T(8,128)S(1)}, u32[]{:S(2)}) copy-start(f32[1792,256]{1,0:T(8,128)S(1)} %constant_dynamic-update-slice_fusion.13) | copy-start | bytes 5505028
  233.0 94.4 %reduce-scatter.6.cloned.1.call-start = ((), (), s32[]{:S(2)}) async-start(), calls=%async_computation.16 | async-start | bytes 1179648 | tf_op jit(solution)/shard_map/reduce_scatter | solution.py:66
  289.1 9.1 %collective-permute-start.4 = (f32[256,256]{1,0:T(8,128)S(1)}, f32[256,256]{1,0:T(8,128)S(1)}, u32[]{:S(2)}, u32[]{:S(2)}) collective-permute-start(f32[256,256]{1,0:T(8,128)S(1)} %slice.128), channel_id=1, source_target_pairs={{4,0},{8,4},{12,8},{16,12},{20,16},{24,20},{28,24},{32,28},{36,32}... | collective-permute-start | bytes 786440 | tf_op jit(solution)/shard_map/ppermute | solution.py:44
  298.3 9.7 %collective-permute-start.5 = (f32[256,256]{1,0:T(8,128)S(1)}, f32[256,256]{1,0:T(8,128)S(1)}, u32[]{:S(2)}, u32[]{:S(2)}) collective-permute-start(f32[256,256]{1,0:T(8,128)S(1)} %slice_add_fusion.2), channel_id=1, source_target_pairs={{4,0},{8,4},{12,8},{16,12},{20,16},{24,20},{28,24},{32,28},{36,32}... | collective-permute-start | bytes 786440 | tf_op jit(solution)/shard_map/ppermute | solution.py:44
  308.0 12.5 %collective-permute-start.6 = (f32[256,256]{1,0:T(8,128)S(1)}, f32[256,256]{1,0:T(8,128)S(1)}, u32[]{:S(2)}, u32[]{:S(2)}) collective-permute-start(f32[256,256]{1,0:T(8,128)S(1)} %slice_add_fusion.1), channel_id=1, source_target_pairs={{4,0},{8,4},{12,8},{16,12},{20,16},{24,20},{28,24},{32,28},{36,32}... | collective-permute-start | bytes 786440 | tf_op jit(solution)/shard_map/ppermute | solution.py:44
  313.1 46.2 %all-to-all-start.8 = ((f32[4,64,1536]{2,1,0:T(8,128)}), f32[4,64,1536]{2,1,0:T(8,128)S(1)}, u32[]{:S(2)}, u32[]{:S(2)}) async-start(f32[4,64,1536]{2,1,0:T(8,128)} %all_to_all.74), calls=%async_computation.8 | async-start | bytes 3145728 | tf_op jit(solution)/shard_map/all_to_all | solution.py:245
  320.5 36.6 %reduce-scatter.8.cloned.1.call-start = ((), (), s32[]{:S(2)}) async-start(), calls=%async_computation.17 | async-start | bytes 196608 | tf_op jit(solution)/shard_map/reduce_scatter | solution.py:66
  321.5 9.9 %collective-permute-start.7 = (f32[256,256]{1,0:T(8,128)S(1)}, f32[256,256]{1,0:T(8,128)S(1)}, u32[]{:S(2)}, u32[]{:S(2)}) collective-permute-start(f32[256,256]{1,0:T(8,128)S(1)} %slice_add_fusion), channel_id=1, source_target_pairs={{4,0},{8,4},{12,8},{16,12},{20,16},{24,20},{28,24},{32,28},{36,32}... | collective-permute-start | bytes 786440 | tf_op jit(solution)/shard_map/ppermute | solution.py:44
  359.3 7.4 %all-to-all-start.10 = ((f32[4,64,128]{2,1,0:T(8,128)}), f32[4,64,128]{2,1,0:T(8,128)S(1)}, u32[]{:S(2)}, u32[]{:S(2)}) async-start(f32[4,64,128]{2,1,0:T(8,128)} %bitcast.37), calls=%async_computation.13 | async-start | bytes 262144 | tf_op jit(solution)/shard_map/all_to_all | solution.py:247
  366.6 7.9 %all-to-all-start.9 = ((f32[4,64,128]{2,1,0:T(8,128)}), f32[4,64,128]{2,1,0:T(8,128)S(1)}, u32[]{:S(2)}, u32[]{:S(2)}) async-start(f32[4,64,128]{2,1,0:T(8,128)} %bitcast.35), calls=%async_computation.12 | async-start | bytes 262144 | tf_op jit(solution)/shard_map/all_to_all | solution.py:246
  (12 other events, 23.4 us)
Sparse Core Ops, SparseCore 0:
  62.3 41.5 all-gather.2
  233.1 55.9 reduce-scatter.3
  291.8 35.5 reduce-scatter.5
  329.8 27.2 reduce-scatter.7
where the time goes:
time: 384 us; the launch traced here: 382 us
  waiting for transfers between devices  120 us (31%)
  starting transfers between devices  73.9 us (19%)
  matrix products  57.4 us (15%)
  local copies, waits for them, and re-layouts  45.2 us (12%)
  between operations  41.9 us (11%)
  blocking collectives  28.2 us (7%)
  other arithmetic  14.8 us (4%)
    reduce_scatter x3, waiting for transfers between devices, own_block(): parts = lax.psum_scatter(parts, axes[k], scatter_dimension=0, tiled=True)  85.3 us
    all_to_all x8, starting transfers between devices, exchange_in_order(): lax.all_to_all(parts, axes[k], split_axis=k, concat_axis=k, tiled=True)  40.9 us
    all_gather x2, blocking collectives, stacked_from(): parts = lax.all_gather(parts, axes[k], axis=0, tiled=True)  28.2 us
    ppermute x8, waiting for transfers between devices, passed_along(): lax.ppermute(value, axis, [(source, source + steps) for source in range(f...  22.9 us
    dot_general x6, matrix products, attend(): jnp.einsum('htk,htd->kd', weights_low, grad_block, preferred_element_type...  19.2 us
    ppermute x8, starting transfers between devices, passed_along(): lax.ppermute(value, axis, [(source, source + steps) for source in range(f...  17.3 us
    dot_general x6, matrix products, attend(): jnp.einsum('htk,htd->kd', grad_scores, query_block, preferred_element_typ...  12.5 us
    dot_general x6, matrix products, attend(): jnp.einsum('htd,kd->htk', query_block, key_matrix, preferred_element_type...  11.9 us
  transfers between devices with their start and end apart: 23, of which 12 were waited for; matrix products, arithmetic and copies ran while one was open for 9% of the time, Pallas kernels for 0%

commit v1 on v0

v1 whole, which is shorter than its diff:
```python
import functools
import math

import jax
import jax.numpy as jnp
from jax import lax
from jax.experimental import pallas as pl
from jax.experimental.pallas import tpu as pltpu
from jax.sharding import Mesh
from jax.sharding import PartitionSpec as P

WIN = 1024
HDR = 64
TOK = 256
BLK = 64
D = 128
HEADS = 12
GROUPS = 4
REACH = WIN // TOK
QB = TOK // BLK
IMPORTS = 4
NX, NY, NZ = 2, 4, 8
NCTX = NX * NY * NZ
WROWS = WIN + BLK
HROWS = IMPORTS * HDR
ROWS = WROWS + HROWS
CHUNK_HEADS = 4
CHUNKS = HEADS // CHUNK_HEADS
CW = CHUNK_HEADS * BLK
COLS = HEADS * BLK
SCALE = 1.0 / math.sqrt(D)
LOG2E = 1.4426950408889634
HIDDEN = -1e30
MESH = pl.DeviceIdType.MESH
F32 = jnp.float32
BF16 = jnp.bfloat16
AXES = ("ctx_0", "ctx_1", "ctx_2", "head_0", "head_1")


def position():
    return tuple(lax.axis_index(a) for a in AXES)


def ctx_of(xh, y, z):
    return xh * (NY * NZ) + y * NZ + z


def ctx_shifted(xh, y, z, step):
    c = lax.rem(ctx_of(xh, y, z) + (NCTX + step), NCTX)
    return {
        "ctx_0": lax.div(c, NY * NZ),
        "ctx_1": lax.rem(lax.div(c, NZ), NY),
        "ctx_2": lax.rem(c, NZ),
    }


def head_peer(xl, co, d):
    pxl = 1 - xl if d & 2 else xl
    pco = 1 - co if d & 1 else co
    return {"head_0": pxl, "head_1": pco}, pxl * 2 + pco


def greet(peers):
    barrier = pltpu.get_barrier_semaphore()
    for peer in peers:
        pl.semaphore_signal(barrier, inc=1, device_id=peer, device_id_type=MESH)
    pl.semaphore_wait(barrier, len(peers))


def remote(src, dst, send, recv, peer):
    return pltpu.make_async_remote_copy(
        src_ref=src, dst_ref=dst, send_sem=send, recv_sem=recv, device_id=peer, device_id_type=MESH
    )


def all_peers(xh, y, z, xl, co):
    peers = [head_peer(xl, co, d)[0] for d in (1, 2, 3)]
    peers += [{"ctx_2": lax.rem(z + d, NZ)} for d in range(1, NZ)]
    peers += [{"ctx_1": lax.rem(y + d, NY)} for d in range(1, NY)]
    peers += [{"ctx_0": 1 - xh}]
    peers += [ctx_shifted(xh, y, z, 1), ctx_shifted(xh, y, z, -1)]
    return peers


def rows(start, size):
    return pl.ds(pl.multiple_of(start, size), size)


def entry_kernel(
    starts, q, k, v, do,
    q_out, do_out, kvwin, slots,
    hsend, hrecv, qsend, qrecv, local, wsend, wrecv, zsend, zrecv, xsend, xrecv, ysend, yrecv,
):
    xh, y, z, xl, co = position()
    me = xl * 2 + co
    width = HEADS * D
    greet(all_peers(xh, y, z, xl, co))
    own = REACH * TOK
    kv_copies, q_copies = [], []
    for d in (1, 2, 3):
        peer, a = head_peer(xl, co, d)
        for n, src in enumerate((k, v)):
            kv_copies.append(remote(
                src.at[:, rows(a * D, D)],
                kvwin.at[rows(own + me * BLK, BLK), pl.ds(n * D, D)],
                hsend.at[d - 1, n], hrecv.at[d - 1, n], peer,
            ))
            kv_copies[-1].start()
    for d in (2, 3, 1):
        peer, a = head_peer(xl, co, d)
        for n, (src, dst) in enumerate(((q, q_out), (do, do_out))):
            q_copies.append(remote(
                src.at[:, rows(a * width, width)], dst.at[rows(me * BLK, BLK), :],
                qsend.at[d - 1, n], qrecv.at[d - 1, n], peer,
            ))
            q_copies[-1].start()
    own_copies = []
    for n, (src, dst) in enumerate(((q, q_out), (do, do_out))):
        own_copies.append(pltpu.make_async_copy(
            src.at[:, rows(me * width, width)], dst.at[rows(me * BLK, BLK), :], local.at[n]
        ))
        own_copies[-1].start()
    for n, src in enumerate((k, v)):
        kvwin[rows(own + me * BLK, BLK), pl.ds(n * D, D)] = src[:, rows(me * D, D)]
    base = ctx_of(xh, y, z) * TOK
    offset = jnp.int32(0)
    for f in range(starts.shape[0]):
        at = starts[f] - base
        offset = offset + jnp.where((at >= 0) & (at < TOK), at, 0)
    for copy in kv_copies:
        copy.wait_recv()

    forward = ctx_shifted(xh, y, z, 1)

    def window_copy(step):
        return remote(
            kvwin.at[pl.ds((REACH + 1 - step) * TOK, TOK), :],
            kvwin.at[pl.ds((REACH - step) * TOK, TOK), :],
            wsend.at[step - 1], wrecv.at[step - 1], forward,
        )

    mine = (y * NX + xh) * NZ + z
    header = jnp.zeros((HDR, 2 * D), F32)
    for b in range(QB):
        keep = jnp.where(offset == b * BLK, 1.0, 0.0)
        header = header + kvwin[own + b * BLK:own + (b + 1) * BLK, :].astype(F32) * keep
    slots[rows(mine * HDR, HDR), :] = header.astype(BF16)
    z_copies = []
    for d in (1, 7, 2, 6, 3, 5, 4):
        z_copies.append(remote(
            slots.at[rows(mine * HDR, HDR), :], slots.at[rows(mine * HDR, HDR), :],
            zsend.at[d - 1], zrecv.at[d - 1], {"ctx_2": lax.rem(z + d, NZ)},
        ))
        z_copies[-1].start()
    w_copies = [window_copy(s) for s in range(1, REACH + 1)]
    w_copies[0].start()
    for copy in z_copies:
        copy.wait_recv()
    line = rows((y * NX + xh) * NZ * HDR, NZ * HDR)
    x_copy = remote(slots.at[line, :], slots.at[line, :], xsend, xrecv, {"ctx_0": 1 - xh})
    x_copy.start()
    w_copies[0].wait_recv()
    w_copies[1].start()
    x_copy.wait_recv()
    plane = rows(y * NX * NZ * HDR, NX * NZ * HDR)
    y_copies = []
    for d in (1, 3, 2):
        y_copies.append(remote(
            slots.at[plane, :], slots.at[plane, :],
            ysend.at[d - 1], yrecv.at[d - 1], {"ctx_1": lax.rem(y + d, NY)},
        ))
        y_copies[-1].start()
    w_copies[1].wait_recv()
    w_copies[2].start()
    w_copies[2].wait_recv()
    w_copies[3].start()
    w_copies[3].wait_recv()
    for copy in q_copies + y_copies:
        copy.wait_recv()
    for copy in own_copies:
        copy.wait()
    for copy in kv_copies + q_copies + z_copies + w_copies + [x_copy] + y_copies:
        copy.wait_send()


def entry(starts, q, k, v, do):
    dma = pltpu.SemaphoreType.DMA
    hbm = pl.BlockSpec(memory_space=pl.ANY)
    vmem = pl.BlockSpec(memory_space=pltpu.VMEM)
    smem = pl.BlockSpec(memory_space=pltpu.SMEM)
    return pl.pallas_call(
        entry_kernel,
        out_shape=(
            jax.ShapeDtypeStruct((TOK, HEADS * D), BF16),
            jax.ShapeDtypeStruct((TOK, HEADS * D), BF16),
            jax.ShapeDtypeStruct(((REACH + 1) * TOK, 2 * D), BF16),
            jax.ShapeDtypeStruct((NCTX * HDR, 2 * D), BF16),
        ),
        in_specs=[smem, hbm, vmem, vmem, hbm],
        out_specs=(hbm, hbm, vmem, vmem),
        scratch_shapes=[
            dma((3, 2)), dma((3, 2)), dma((3, 2)), dma((3, 2)), dma((2,)),
            dma((REACH,)), dma((REACH,)), dma((NZ - 1,)), dma((NZ - 1,)),
            dma, dma, dma((NY - 1,)), dma((NY - 1,)),
        ],
        compiler_params=pltpu.CompilerParams(
            collective_id=0, has_side_effects=True, vmem_limit_bytes=32 * 2**20
        ),
        name="entry",
    )(starts, q, k, v, do)


def fold8(x, op):
    out = x[0:8]
    for r in range(8, x.shape[0], 8):
        out = op(out, x[r:r + 8])
    return out


def file_at(starts, place):
    count = jnp.int32(-1)
    for f in range(starts.shape[0]):
        count = count + jnp.where(starts[f] <= place, 1, 0)
    return count


def slot_of(start):
    c = lax.div(start, TOK)
    xh = lax.div(c, NY * NZ)
    y = lax.rem(lax.div(c, NZ), NY)
    z = lax.rem(c, NZ)
    return (y * NX + xh) * NZ + z


def compute_kernel(
    starts, imports, lens, q, do, kvwin, slots,
    dq_out, dkv, table,
    kc, vc, bias, qs, dos, s_ref, dp_ref, p_ref, ds_ref, hacc,
):
    xh, y, z, _, _ = position()
    base = ctx_of(xh, y, z) * TOK
    lower = file_at(starts, base)
    upper = file_at(starts, base + TOK - 1)
    dkv[...] = jnp.zeros_like(dkv)
    hacc[...] = jnp.zeros_like(hacc)
    table[...] = jnp.zeros_like(table)
    step = 64

    def one_block(qb, carry):
        place = base + qb * BLK
        file = file_at(starts, place)
        begin = starts[file]
        kc[0:WROWS, :] = kvwin[rows_at(qb * BLK, WROWS, BLK), 0:D]
        vc[0:WROWS, :] = kvwin[rows_at(qb * BLK, WROWS, BLK), D:2 * D]
        key_place = lax.broadcasted_iota(jnp.int32, (WROWS, D), 0) + (place - WIN)
        bias[0:WROWS, :] = jnp.where(key_place >= begin, 0.0, HIDDEN)
        offsets = lax.broadcasted_iota(jnp.int32, (HDR, D), 0)
        for m in range(IMPORTS):
            g = imports[file, m]
            known = jnp.maximum(g, 0)
            length = jnp.where(g >= 0, lens[known], 0)
            at = rows(slot_of(starts[known]) * HDR, HDR)
            here = pl.ds(WROWS + m * HDR, HDR)
            kc[here, :] = slots[at, 0:D]
            vc[here, :] = slots[at, D:2 * D]
            bias[here, :] = jnp.where(offsets < length, 0.0, HIDDEN)
        for h in range(HEADS):
            qs[h * BLK:(h + 1) * BLK, :] = q[rows(qb * BLK, BLK), h * D:(h + 1) * D]
            dos[h * BLK:(h + 1) * BLK, :] = do[rows(qb * BLK, BLK), h * D:(h + 1) * D]

        t = lax.broadcasted_iota(jnp.int32, (BLK, CW), 0)
        p_at = lax.broadcasted_iota(jnp.int32, (BLK, CW), 1) % BLK
        nt = (((1,), (1,)), ((), ()))
        for chunk in range(CHUNKS):
            cols = slice(chunk * CW, (chunk + 1) * CW)
            s_ref[...] = lax.dot_general(kc[...], qs[cols, :], nt, preferred_element_type=F32)
            dp_ref[...] = lax.dot_general(vc[...], dos[cols, :], nt, preferred_element_type=F32)
            top = None
            for r in range(0, ROWS, step):
                b = bias[r:r + step, :]
                s = s_ref[r:r + step, :] + jnp.concatenate([b] * (CW // D), axis=1)
                if r == 0:
                    s = jnp.where(t > p_at, s, HIDDEN)
                if r == WIN:
                    s = jnp.where(t <= p_at, s, HIDDEN)
                s_ref[r:r + step, :] = s
                part = fold8(s, jnp.maximum)
                top = part if top is None else jnp.maximum(top, part)
            top = jnp.max(top, axis=0, keepdims=True)
            total = jnp.zeros((8, CW), F32)
            centre = jnp.zeros((8, CW), F32)
            for r in range(0, ROWS, step):
                e = jnp.exp2((s_ref[r:r + step, :] - top) * (SCALE * LOG2E))
                s_ref[r:r + step, :] = e
                total = total + fold8(e, jnp.add)
                centre = centre + fold8(e * dp_ref[r:r + step, :], jnp.add)
            inverse = 1.0 / jnp.sum(total, axis=0, keepdims=True)
            centre = jnp.sum(centre, axis=0, keepdims=True) * inverse
            for r in range(0, ROWS, step):
                w = s_ref[r:r + step, :] * inverse
                p_ref[r:r + step, cols] = w.astype(BF16)
                ds_ref[r:r + step, cols] = (w * (dp_ref[r:r + step, :] - centre)).astype(BF16)
        dv = jnp.dot(p_ref[...], dos[...], preferred_element_type=F32)
        dk = jnp.dot(ds_ref[...], qs[...], preferred_element_type=F32) * SCALE
        window = rows_at(qb * BLK, WROWS, BLK)
        dkv[window, 0:D] += dk[0:WROWS]
        dkv[window, D:2 * D] += dv[0:WROWS]
        which = jnp.where(file == lower, 0, 1)
        hdr = rows(which * HROWS, HROWS)
        hacc[hdr, 0:D] += dk[WROWS:]
        hacc[hdr, D:2 * D] += dv[WROWS:]
        dqt = lax.dot_general(
            kc[...], ds_ref[...], (((0,), (0,)), ((), ())), preferred_element_type=F32
        )
        dq = (dqt.T * SCALE).astype(BF16)
        for h in range(HEADS):
            dq_out[rows(qb * BLK, BLK), h * D:(h + 1) * D] = dq[h * BLK:(h + 1) * BLK]
        return carry

    lax.fori_loop(0, QB, one_block, 0)
    for which, file in ((0, lower), (1, upper)):
        for m in range(IMPORTS):
            g = imports[file, m]
            usable = g >= 0 if which == 0 else (g >= 0) & (upper != lower)

            @pl.when(usable)
            def _():
                at = rows(slot_of(starts[jnp.maximum(g, 0)]) * HDR, HDR)
                part = hacc[pl.ds((which * IMPORTS + m) * HDR, HDR), :]
                table[at, :] = (table[at, :].astype(F32) + part).astype(BF16)


def rows_at(start, size, multiple):
    return pl.ds(pl.multiple_of(start, multiple), size)


def compute(starts, imports, lens, q, do, kvwin, slots):
    vmem = pl.BlockSpec(memory_space=pltpu.VMEM)
    smem = pl.BlockSpec(memory_space=pltpu.SMEM)
    return pl.pallas_call(
        compute_kernel,
        out_shape=(
            jax.ShapeDtypeStruct((TOK, HEADS * D), BF16),
            jax.ShapeDtypeStruct(((REACH + 1) * TOK, 2 * D), F32),
            jax.ShapeDtypeStruct((NCTX * HDR, 2 * D), BF16),
        ),
        in_specs=[smem, smem, smem, vmem, vmem, vmem, vmem],
        out_specs=(vmem, vmem, vmem),
        scratch_shapes=[
            pltpu.VMEM((ROWS, D), BF16), pltpu.VMEM((ROWS, D), BF16), pltpu.VMEM((ROWS, D), F32),
            pltpu.VMEM((COLS, D), BF16), pltpu.VMEM((COLS, D), BF16),
            pltpu.VMEM((ROWS, CW), F32), pltpu.VMEM((ROWS, CW), F32),
            pltpu.VMEM((ROWS, COLS), BF16), pltpu.VMEM((ROWS, COLS), BF16),
            pltpu.VMEM((2 * HROWS, 2 * D), F32),
        ],
        compiler_params=pltpu.CompilerParams(vmem_limit_bytes=48 * 2**20),
        name="attend",
    )(starts, imports, lens, q, do, kvwin, slots)


def exit_kernel(
    starts, dq, dkv, table,
    dq_out, dk_out, dv_out,
    ry, tx, rx, acc, tz, rz, wout, win, coll,
    ysend, yrecv, qsend, qrecv, local, wsend, wrecv, xsend, xrecv, zsend, zrecv, hsend, hrecv,
):
    xh, y, z, xl, co = position()
    me = xl * 2 + co
    width = HEADS * D
    greet(all_peers(xh, y, z, xl, co))
    plane = NX * NZ * HDR
    line = NZ * HDR
    y_copies = []
    for d in (1, 3, 2):
        to = lax.rem(y + d, NY)
        y_copies.append(remote(
            table.at[rows(to * plane, plane), :], ry.at[d - 1],
            ysend.at[d - 1], yrecv.at[d - 1], {"ctx_1": to},
        ))
        y_copies[-1].start()
    back = ctx_shifted(xh, y, z, -1)
    w_copies = [
        remote(wout.at[s], win.at[s], wsend.at[s], wrecv.at[s], back) for s in range(REACH)
    ]
    wout[0] = dkv[0:TOK, :].astype(BF16)
    w_copies[0].start()
    q_copies = []
    for d in (2, 3, 1):
        peer, a = head_peer(xl, co, d)
        q_copies.append(remote(
            dq.at[rows(a * BLK, BLK), :], dq_out.at[:, rows(me * width, width)],
            qsend.at[d - 1], qrecv.at[d - 1], peer,
        ))
        q_copies[-1].start()
    own = pltpu.make_async_copy(
        dq.at[rows(me * BLK, BLK), :], dq_out.at[:, rows(me * width, width)], local
    )
    own.start()
    for s in range(1, REACH):
        w_copies[s - 1].wait_recv()
        wout[s] = (win[s - 1].astype(F32) + dkv[s * TOK:(s + 1) * TOK, :]).astype(BF16)
        w_copies[s].start()
    for copy in y_copies:
        copy.wait_recv()

    def plane_sum(block):
        at = rows(block * line, line)
        total = table[rows(y * plane + block * line, line), :].astype(F32)
        for d in range(NY - 1):
            total = total + ry[d, at, :].astype(F32)
        return total

    tx[...] = plane_sum(1 - xh).astype(BF16)
    x_copy = remote(tx, rx, xsend, xrecv, {"ctx_0": 1 - xh})
    x_copy.start()
    acc[...] = plane_sum(xh)
    x_copy.wait_recv()
    acc[...] += rx[...].astype(F32)
    tz[...] = acc[...].astype(BF16)
    z_copies = []
    for d in (4, 3, 5, 2, 6, 1, 7):
        to = lax.rem(z + d, NZ)
        z_copies.append(remote(
            tz.at[rows(to * HDR, HDR), :], rz.at[d - 1],
            zsend.at[d - 1], zrecv.at[d - 1], {"ctx_2": to},
        ))
        z_copies[-1].start()
    w_copies[REACH - 1].wait_recv()
    header = acc[rows(z * HDR, HDR), :]
    for copy in z_copies:
        copy.wait_recv()
    for d in range(NZ - 1):
        header = header + rz[d].astype(F32)
    base = ctx_of(xh, y, z) * TOK
    offset = jnp.int32(0)
    for f in range(starts.shape[0]):
        at = starts[f] - base
        offset = offset + jnp.where((at >= 0) & (at < TOK), at, 0)
    for b in range(QB):
        part = slice(b * BLK, (b + 1) * BLK)
        keep = jnp.where(offset == b * BLK, 1.0, 0.0)
        coll[part, :] = (
            dkv[REACH * TOK + b * BLK:REACH * TOK + (b + 1) * BLK, :]
            + win[REACH - 1, part, :].astype(F32)
            + header * keep
        )
    h_copies = []
    for d in (2, 3, 1):
        peer, a = head_peer(xl, co, d)
        for n, dst in enumerate((dk_out, dv_out)):
            h_copies.append(remote(
                coll.at[rows(a * BLK, BLK), pl.ds(n * D, D)], dst.at[:, rows(me * D, D)],
                hsend.at[d - 1, n], hrecv.at[d - 1, n], peer,
            ))
            h_copies[-1].start()
    for n, dst in enumerate((dk_out, dv_out)):
        dst[:, rows(me * D, D)] = coll[rows(me * BLK, BLK), n * D:(n + 1) * D]
    own.wait()
    for copy in q_copies + h_copies:
        copy.wait_recv()
    for copy in y_copies + w_copies + q_copies + [x_copy] + z_copies + h_copies:
        copy.wait_send()


def leave(starts, dq, dkv, table):
    dma = pltpu.SemaphoreType.DMA
    hbm = pl.BlockSpec(memory_space=pl.ANY)
    vmem = pl.BlockSpec(memory_space=pltpu.VMEM)
    smem = pl.BlockSpec(memory_space=pltpu.SMEM)
    plane = NX * NZ * HDR
    line = NZ * HDR
    return pl.pallas_call(
        exit_kernel,
        out_shape=(
            jax.ShapeDtypeStruct((BLK, GROUPS * HEADS * D), BF16),
            jax.ShapeDtypeStruct((BLK, GROUPS * D), F32),
            jax.ShapeDtypeStruct((BLK, GROUPS * D), F32),
        ),
        in_specs=[smem, hbm, vmem, vmem],
        out_specs=(hbm, vmem, vmem),
        scratch_shapes=[
            pltpu.VMEM((NY - 1, plane, 2 * D), BF16),
            pltpu.VMEM((line, 2 * D), BF16), pltpu.VMEM((line, 2 * D), BF16),
            pltpu.VMEM((line, 2 * D), F32), pltpu.VMEM((line, 2 * D), BF16),
            pltpu.VMEM((NZ - 1, HDR, 2 * D), BF16),
            pltpu.VMEM((REACH, TOK, 2 * D), BF16), pltpu.VMEM((REACH, TOK, 2 * D), BF16),
            pltpu.VMEM((TOK, 2 * D), F32),
            dma((NY - 1,)), dma((NY - 1,)), dma((3,)), dma((3,)), dma,
            dma((REACH,)), dma((REACH,)), dma, dma, dma((NZ - 1,)), dma((NZ - 1,)),
            dma((3, 2)), dma((3, 2)),
        ],
        compiler_params=pltpu.CompilerParams(
            collective_id=1, has_side_effects=True, vmem_limit_bytes=32 * 2**20
        ),
        name="leave",
    )(starts, dq, dkv, table)


def per_device(queries, keys, values, output_gradient, file_starts, file_imports, header_lens):
    q, do, kvwin, slots = entry(file_starts, queries, keys, values, output_gradient)
    dq, dkv, table = compute(file_starts, file_imports, header_lens, q, do, kvwin, slots)
    dq_low, dk, dv = leave(file_starts, dq, dkv, table)
    return dq_low.astype(F32), dk, dv


def solution(mesh):
    split = Mesh(mesh.devices.reshape(NX, NY, NZ, 2, 2), AXES)
    placed = P(AXES, None)
    return jax.shard_map(
        per_device,
        mesh=split,
        in_specs=(placed, placed, placed, placed, P(), P(), P()),
        out_specs=(placed, placed, placed),
        check_vma=False,
    )
```

time: 384 us -> 159 us (0.41)
  the two profiles are of different devices: /device:TPU:1 before, /device:TPU:9 now
where the time goes in v1:
time: 159 us
  Pallas kernels  146 us (92%)
  local copies, waits for them, and re-layouts  10.9 us (7%)
    pallas_call x1, Pallas kernels, entry(): pl.pallas_call(entry_kernel, out_shape=(jax.ShapeDtypeStruct((TOK, HEADS...  70 us
    pallas_call x1, Pallas kernels, leave(): pl.pallas_call(exit_kernel, out_shape=(jax.ShapeDtypeStruct((BLK, GROUPS...  55.9 us
    pallas_call x1, Pallas kernels, compute(): pl.pallas_call(compute_kernel, out_shape=(jax.ShapeDtypeStruct((TOK, HEAD...  19.8 us
    unnamed x21, local copies, waits for them, and re-layouts  10.9 us

profile of v1, /device:TPU:9, one launch (start us, length us, event | category | flops | bytes accessed | tf_op | source)
XLA Modules:
  0.0 158.5 jit_solution(12950789277903287962)
XLA Ops:
  0.6 0.8 copy.10.imports
  1.4 0.0 copy-start.2
  1.4 1.1 copy-done.2
  2.5 0.0 copy-start.3
  2.5 1.1 copy-done.3
  3.7 0.0 copy-start.4
  3.7 0.8 copy-done.4
  4.5 0.0 copy-start.5
  4.5 0.8 copy-done.5
  5.4 0.0 copy-start.6
  5.4 0.7 copy-done.6
  6.0 70.0 %entry.1 = (bf16[256,1536]{1,0:T(8,128)(2,1)S(1)}, bf16[256,1536]{1,0:T(8,128)(2,1)S(1)}, bf16[1280,256]{1,0:T(8,128)(2,1)S(1)}, bf16[4096,256]{1,0:T(8,128)(2,1)S(1)}) custom-call(s32[33]{0:T(128)S(1)} %copy-done.6, bf16[64,6144]{1,0:T(8,128)(2,1)S(1)} %copy-done.2, bf16[64,512]{1,0:T(8,128)(2,1)S(1)} %copy-done.4, bf16[64,512]{1,0:T(8,128)(2,1)S(1)} %copy-done.5, ...), custom_call_target="tpu_custom_call" | custom-call | tf_op jit(solution)/shard_map/entry/pallas_call | solution.py:191
  76.0 0.0 copy-start.1
  76.0 1.3 copy-done.1
  77.3 0.0 copy-start.7
  77.3 0.7 copy-done.7
  78.0 0.0 copy-start.8
  78.0 0.7 copy-done.8
  78.6 19.8 %attend.1 = (bf16[256,1536]{1,0:T(8,128)(2,1)S(1)}, f32[1280,256]{1,0:T(8,128)S(1)}, bf16[4096,256]{1,0:T(8,128)(2,1)}) custom-call(s32[33]{0:T(128)S(1)} %copy-done.7, s32[33,4]{1,0:T(8,128)S(1)} %copy.10.imports, s32[33]{0:T(128)S(1)} %copy-done.8, bf16[256,1536]{1,0:T(8,128)(2,1)S(1)} %get-tuple-element.13.q, bf16[256,1536]{1,0:T(8,128)(2,1)S(1)} %get-tuple-element.14.do, ...), custom_call_target="tpu_custom_call" | custom-call | tf_op jit(solution)/shard_map/attend/pallas_call | solution.py:340
  98.4 0.0 copy-start
  98.4 1.6 %copy-done = bf16[4096,256]{1,0:T(8,128)(2,1)S(1)} copy-done((bf16[4096,256]{1,0:T(8,128)(2,1)S(1)}, bf16[4096,256]{1,0:T(8,128)(2,1)}, u32[]{:S(2)}) %copy-start) | copy-done | bytes 2097176
  100.0 55.9 %leave.1 = (bf16[64,6144]{1,0:T(8,128)(2,1)S(1)}, f32[64,512]{1,0:T(8,128)S(1)}, f32[64,512]{1,0:T(8,128)S(1)}) custom-call(s32[33]{0:T(128)S(1)} %copy-done.7, bf16[256,1536]{1,0:T(8,128)(2,1)S(1)} %get-tuple-element.17.dq, f32[1280,256]{1,0:T(8,128)S(1)} %get-tuple-element.18.dkv, bf16[4096,256]{1,0:T(8,128)(2,1)S(1)} %copy-done), custom_call_target="tpu_custom_call" | custom-call | tf_op jit(solution)/shard_map/leave/pallas_call | solution.py:472
  155.9 1.2 convert_element_type.3
  157.2 0.7 copy.13
  157.8 0.7 copy.14
Async XLA Ops:
  1.4 1.1 copy-start.2
  2.5 1.1 copy-start.3
  3.7 0.8 copy-start.4
  4.5 0.8 copy-start.5
  5.4 0.7 copy-start.6
  76.0 1.3 copy-start.1
  77.3 0.7 copy-start.7
  78.0 0.7 copy-start.8
  98.4 1.6 %copy-start = (bf16[4096,256]{1,0:T(8,128)(2,1)S(1)}, bf16[4096,256]{1,0:T(8,128)(2,1)}, u32[]{:S(2)}) copy-start(bf16[4096,256]{1,0:T(8,128)(2,1)} %get-tuple-element.19.table) | copy-start | bytes 6291460

commit v2 on v1

v2 whole, which is shorter than its diff:
```python
import functools
import math

import jax
import jax.numpy as jnp
from jax import lax
from jax.experimental import pallas as pl
from jax.experimental.pallas import tpu as pltpu
from jax.sharding import Mesh
from jax.sharding import PartitionSpec as P

WIN = 1024
HDR = 64
TOK = 256
BLK = 64
D = 128
HEADS = 12
GROUPS = 4
REACH = WIN // TOK
QB = TOK // BLK
IMPORTS = 4
NX, NY, NZ = 2, 4, 8
NCTX = NX * NY * NZ
WROWS = WIN + BLK
HROWS = IMPORTS * HDR
ROWS = WROWS + HROWS
CHUNK_HEADS = 4
CHUNKS = HEADS // CHUNK_HEADS
CW = CHUNK_HEADS * BLK
COLS = HEADS * BLK
SCALE = 1.0 / math.sqrt(D)
LOG2E = 1.4426950408889634
HIDDEN = -1e30
MESH = pl.DeviceIdType.MESH
F32 = jnp.float32
BF16 = jnp.bfloat16
AXES = ("ctx_0", "ctx_1", "ctx_2", "head_0", "head_1")


def position():
    return tuple(lax.axis_index(a) for a in AXES)


def ctx_of(xh, y, z):
    return xh * (NY * NZ) + y * NZ + z


def ctx_shifted(xh, y, z, step):
    c = lax.rem(ctx_of(xh, y, z) + (NCTX + step), NCTX)
    return {
        "ctx_0": lax.div(c, NY * NZ),
        "ctx_1": lax.rem(lax.div(c, NZ), NY),
        "ctx_2": lax.rem(c, NZ),
    }


def head_peer(xl, co, d):
    pxl = 1 - xl if d & 2 else xl
    pco = 1 - co if d & 1 else co
    return {"head_0": pxl, "head_1": pco}, pxl * 2 + pco


def greet(peers):
    barrier = pltpu.get_barrier_semaphore()
    for peer in peers:
        pl.semaphore_signal(barrier, inc=1, device_id=peer, device_id_type=MESH)
    pl.semaphore_wait(barrier, len(peers))


def remote(src, dst, send, recv, peer):
    return pltpu.make_async_remote_copy(
        src_ref=src, dst_ref=dst, send_sem=send, recv_sem=recv, device_id=peer, device_id_type=MESH
    )


def all_peers(xh, y, z, xl, co):
    peers = [head_peer(xl, co, d)[0] for d in (1, 2, 3)]
    peers += [{"ctx_2": lax.rem(z + d, NZ)} for d in range(1, NZ)]
    peers += [{"ctx_1": n} for n in y_neighbours(y)]
    peers += [{"ctx_0": 1 - xh}]
    peers += [ctx_shifted(xh, y, z, 1), ctx_shifted(xh, y, z, -1)]
    return peers


def rows(start, size):
    return pl.ds(pl.multiple_of(start, size), size)


def y_neighbours(y):
    near = y + 1 - 2 * lax.rem(y, 2)
    return near, NY - 1 - y


def file_at(starts, place):
    count = jnp.int32(-1)
    for f in range(starts.shape[0]):
        count = count + jnp.where(starts[f] <= place, 1, 0)
    return count


def header_blocks(starts, imports, c):
    lower = file_at(starts, c * TOK)
    upper = file_at(starts, c * TOK + TOK - 1)
    blocks = []
    for file in (lower, upper):
        for m in range(IMPORTS):
            g = imports[file, m]
            blocks.append((g >= 0, lax.div(starts[jnp.maximum(g, 0)], TOK)))
    return lower, upper, blocks


def own_header_offset(starts, base):
    offset = jnp.int32(0)
    for f in range(starts.shape[0]):
        at = starts[f] - base
        offset = offset + jnp.where((at >= 0) & (at < TOK), at, 0)
    return offset


def fetch(pairs, sems):
    copies = [pltpu.make_async_copy(src, dst, sems.at[n]) for n, (src, dst) in enumerate(pairs)]
    for copy in copies:
        copy.start()
    return copies


def entry_kernel(
    starts_hbm, imports_hbm, q, k, v, do,
    q_out, do_out, kvwin, slots, far,
    starts, imports, picked,
    fsem, hsend, hrecv, qsend, qrecv, local, wsend, wrecv, zsend, zrecv, xsend, xrecv,
    ysend, yrecv,
):
    xh, y, z, xl, co = position()
    me = xl * 2 + co
    c = ctx_of(xh, y, z)
    width = HEADS * D
    own = REACH * TOK
    small = fetch(((starts_hbm, starts), (imports_hbm, imports)), fsem)
    here = fetch(
        (
            (k.at[:, rows(me * D, D)], kvwin.at[rows(own + me * BLK, BLK), pl.ds(0, D)]),
            (v.at[:, rows(me * D, D)], kvwin.at[rows(own + me * BLK, BLK), pl.ds(D, D)]),
            (q.at[:, rows(me * width, width)], q_out.at[rows(me * BLK, BLK), :]),
            (do.at[:, rows(me * width, width)], do_out.at[rows(me * BLK, BLK), :]),
        ),
        local,
    )
    greet(all_peers(xh, y, z, xl, co))
    kv_copies, q_copies = [], []
    for d in (2, 3, 1):
        peer, a = head_peer(xl, co, d)
        for n, src in enumerate((k, v)):
            kv_copies.append(remote(
                src.at[:, rows(a * D, D)],
                kvwin.at[rows(own + me * BLK, BLK), pl.ds(n * D, D)],
                hsend.at[d - 1, n], hrecv.at[d - 1, n], peer,
            ))
            kv_copies[-1].start()
    for d in (2, 3, 1):
        peer, a = head_peer(xl, co, d)
        for n, (src, dst) in enumerate(((q, q_out), (do, do_out))):
            q_copies.append(remote(
                src.at[:, rows(a * width, width)], dst.at[rows(me * BLK, BLK), :],
                qsend.at[d - 1, n], qrecv.at[d - 1, n], peer,
            ))
            q_copies[-1].start()
    for copy in small:
        copy.wait()
    offset = own_header_offset(starts, c * TOK)
    for copy in here[:2]:
        copy.wait()
    for copy in kv_copies:
        copy.wait_recv()

    forward = ctx_shifted(xh, y, z, 1)
    w_copies = [
        remote(
            kvwin.at[pl.ds((REACH - s) * TOK, TOK), :],
            kvwin.at[pl.ds((REACH - 1 - s) * TOK, TOK), :],
            wsend.at[s], wrecv.at[s], forward,
        )
        for s in range(REACH)
    ]
    header = jnp.zeros((HDR, 2 * D), F32)
    for b in range(QB):
        keep = jnp.where(offset == b * BLK, 1.0, 0.0)
        header = header + kvwin[own + b * BLK:own + (b + 1) * BLK, :].astype(F32) * keep
    line = y * NZ + z
    slots[line] = header.astype(BF16)
    z_copies = []
    for d in (1, 7, 2, 6, 3, 5, 4):
        z_copies.append(remote(
            slots.at[line], slots.at[line],
            zsend.at[d - 1], zrecv.at[d - 1], {"ctx_2": lax.rem(z + d, NZ)},
        ))
        z_copies[-1].start()
    w_copies[0].start()
    for copy in z_copies:
        copy.wait_recv()
    near, other = y_neighbours(y)
    y_copies = []
    for n, to in enumerate((near, other)):
        y_copies.append(remote(
            slots.at[rows(y * NZ, NZ)], slots.at[rows(y * NZ, NZ)],
            ysend.at[n], yrecv.at[n], {"ctx_1": to},
        ))
        y_copies[-1].start()
    w_copies[0].wait_recv()
    w_copies[1].start()
    for n, (came, to) in enumerate(((near, other), (other, near))):
        y_copies[n].wait_recv()
        part = slots.at[rows(came * NZ, NZ), :, pl.ds(n * D, D)]
        y_copies.append(remote(part, part, ysend.at[2 + n], yrecv.at[2 + n], {"ctx_1": to}))
        y_copies[-1].start()
    w_copies[1].wait_recv()
    w_copies[2].start()
    _, _, wanted = header_blocks(starts, imports, ctx_of(1 - xh, y, z))
    for copy in y_copies[2:]:
        copy.wait_recv()
    for m, (_, shard) in enumerate(wanted):
        picked[m] = slots[lax.rem(shard, NY * NZ)]
    x_copy = remote(picked, far, xsend, xrecv, {"ctx_0": 1 - xh})
    x_copy.start()
    w_copies[2].wait_recv()
    w_copies[3].start()
    w_copies[3].wait_recv()
    x_copy.wait_recv()
    for copy in q_copies:
        copy.wait_recv()
    for copy in here[2:]:
        copy.wait()
    for copy in kv_copies + q_copies + z_copies + w_copies + y_copies + [x_copy]:
        copy.wait_send()


def entry(starts, imports, q, k, v, do):
    dma = pltpu.SemaphoreType.DMA
    hbm = pl.BlockSpec(memory_space=pl.ANY)
    vmem = pl.BlockSpec(memory_space=pltpu.VMEM)
    return pl.pallas_call(
        entry_kernel,
        out_shape=(
            jax.ShapeDtypeStruct((TOK, HEADS * D), BF16),
            jax.ShapeDtypeStruct((TOK, HEADS * D), BF16),
            jax.ShapeDtypeStruct(((REACH + 1) * TOK, 2 * D), BF16),
            jax.ShapeDtypeStruct((NY * NZ, HDR, 2 * D), BF16),
            jax.ShapeDtypeStruct((2 * IMPORTS, HDR, 2 * D), BF16),
        ),
        in_specs=[hbm] * 6,
        out_specs=(hbm, hbm, vmem, vmem, vmem),
        scratch_shapes=[
            pltpu.SMEM(starts.shape, jnp.int32), pltpu.SMEM(imports.shape, jnp.int32),
            pltpu.VMEM((2 * IMPORTS, HDR, 2 * D), BF16),
            dma((2,)), dma((3, 2)), dma((3, 2)), dma((3, 2)), dma((3, 2)), dma((4,)),
            dma((REACH,)), dma((REACH,)), dma((NZ - 1,)), dma((NZ - 1,)),
            dma, dma, dma((4,)), dma((4,)),
        ],
        compiler_params=pltpu.CompilerParams(
            collective_id=0, has_side_effects=True, vmem_limit_bytes=32 * 2**20
        ),
        name="entry",
    )(starts, imports, q, k, v, do)


def fold8(x, op):
    out = x[0:8]
    for r in range(8, x.shape[0], 8):
        out = op(out, x[r:r + 8])
    return out


def compute_kernel(
    starts, imports, lens, q, do, kvwin, slots, far,
    dq_out, dkv, packed,
    kc, vc, bias, qs, dos, s_ref, dp_ref, p_ref, ds_ref, hacc,
):
    xh, y, z, _, _ = position()
    base = ctx_of(xh, y, z) * TOK
    lower = file_at(starts, base)
    dkv[...] = jnp.zeros_like(dkv)
    hacc[...] = jnp.zeros_like(hacc)
    step = 64

    def one_block(qb, carry):
        place = base + qb * BLK
        file = file_at(starts, place)
        begin = starts[file]
        kc[0:WROWS, :] = kvwin[rows_at(qb * BLK, WROWS, BLK), 0:D]
        vc[0:WROWS, :] = kvwin[rows_at(qb * BLK, WROWS, BLK), D:2 * D]
        key_place = lax.broadcasted_iota(jnp.int32, (WROWS, D), 0) + (place - WIN)
        bias[0:WROWS, :] = jnp.where(key_place >= begin, 0.0, HIDDEN)
        offsets = lax.broadcasted_iota(jnp.int32, (HDR, D), 0)
        for m in range(IMPORTS):
            g = imports[file, m]
            known = jnp.maximum(g, 0)
            length = jnp.where(g >= 0, lens[known], 0)
            shard = lax.div(starts[known], TOK)
            at = lax.rem(shard, NY * NZ)
            which = jnp.where(file == lower, 0, IMPORTS) + m
            same = jnp.full((HDR, 2 * D), lax.div(shard, NY * NZ)) == xh
            rows_kv = jnp.where(same, slots[at].astype(F32), far[which].astype(F32)).astype(BF16)
            here = pl.ds(WROWS + m * HDR, HDR)
            kc[here, :] = rows_kv[:, 0:D]
            vc[here, :] = rows_kv[:, D:2 * D]
            bias[here, :] = jnp.where(offsets < length, 0.0, HIDDEN)
        for h in range(HEADS):
            qs[h * BLK:(h + 1) * BLK, :] = q[rows(qb * BLK, BLK), h * D:(h + 1) * D]
            dos[h * BLK:(h + 1) * BLK, :] = do[rows(qb * BLK, BLK), h * D:(h + 1) * D]

        t = lax.broadcasted_iota(jnp.int32, (BLK, CW), 0)
        p_at = lax.broadcasted_iota(jnp.int32, (BLK, CW), 1) % BLK
        nt = (((1,), (1,)), ((), ()))
        for chunk in range(CHUNKS):
            cols = slice(chunk * CW, (chunk + 1) * CW)
            s_ref[...] = lax.dot_general(kc[...], qs[cols, :], nt, preferred_element_type=F32)
            dp_ref[...] = lax.dot_general(vc[...], dos[cols, :], nt, preferred_element_type=F32)
            top = None
            for r in range(0, ROWS, step):
                b = bias[r:r + step, :]
                s = s_ref[r:r + step, :] + jnp.concatenate([b] * (CW // D), axis=1)
                if r == 0:
                    s = jnp.where(t > p_at, s, HIDDEN)
                if r == WIN:
                    s = jnp.where(t <= p_at, s, HIDDEN)
                s_ref[r:r + step, :] = s
                part = fold8(s, jnp.maximum)
                top = part if top is None else jnp.maximum(top, part)
            top = jnp.max(top, axis=0, keepdims=True)
            total = jnp.zeros((8, CW), F32)
            centre = jnp.zeros((8, CW), F32)
            for r in range(0, ROWS, step):
                e = jnp.exp2((s_ref[r:r + step, :] - top) * (SCALE * LOG2E))
                s_ref[r:r + step, :] = e
                total = total + fold8(e, jnp.add)
                centre = centre + fold8(e * dp_ref[r:r + step, :], jnp.add)
            inverse = 1.0 / jnp.sum(total, axis=0, keepdims=True)
            centre = jnp.sum(centre, axis=0, keepdims=True) * inverse
            for r in range(0, ROWS, step):
                w = s_ref[r:r + step, :] * inverse
                p_ref[r:r + step, cols] = w.astype(BF16)
                ds_ref[r:r + step, cols] = (w * (dp_ref[r:r + step, :] - centre)).astype(BF16)
        dv = jnp.dot(p_ref[...], dos[...], preferred_element_type=F32)
        dk = jnp.dot(ds_ref[...], qs[...], preferred_element_type=F32) * SCALE
        window = rows_at(qb * BLK, WROWS, BLK)
        dkv[window, 0:D] += dk[0:WROWS]
        dkv[window, D:2 * D] += dv[0:WROWS]
        which = jnp.where(file == lower, 0, 1)
        hdr = rows(which * HROWS, HROWS)
        hacc[hdr, 0:D] += dk[WROWS:]
        hacc[hdr, D:2 * D] += dv[WROWS:]
        dqt = lax.dot_general(
            kc[...], ds_ref[...], (((0,), (0,)), ((), ())), preferred_element_type=F32
        )
        dq = (dqt.T * SCALE).astype(BF16)
        for h in range(HEADS):
            dq_out[rows(qb * BLK, BLK), h * D:(h + 1) * D] = dq[h * BLK:(h + 1) * BLK]
        return carry

    lax.fori_loop(0, QB, one_block, 0)
    for m in range(2 * IMPORTS):
        packed[m] = hacc[m * HDR:(m + 1) * HDR, :].astype(BF16)


def rows_at(start, size, multiple):
    return pl.ds(pl.multiple_of(start, multiple), size)


def compute(starts, imports, lens, q, do, kvwin, slots, far):
    vmem = pl.BlockSpec(memory_space=pltpu.VMEM)
    smem = pl.BlockSpec(memory_space=pltpu.SMEM)
    return pl.pallas_call(
        compute_kernel,
        out_shape=(
            jax.ShapeDtypeStruct((TOK, HEADS * D), BF16),
            jax.ShapeDtypeStruct(((REACH + 1) * TOK, 2 * D), F32),
            jax.ShapeDtypeStruct((2 * IMPORTS, HDR, 2 * D), BF16),
        ),
        in_specs=[smem, smem, smem, vmem, vmem, vmem, vmem, vmem],
        out_specs=(vmem, vmem, vmem),
        scratch_shapes=[
            pltpu.VMEM((ROWS, D), BF16), pltpu.VMEM((ROWS, D), BF16), pltpu.VMEM((ROWS, D), F32),
            pltpu.VMEM((COLS, D), BF16), pltpu.VMEM((COLS, D), BF16),
            pltpu.VMEM((ROWS, CW), F32), pltpu.VMEM((ROWS, CW), F32),
            pltpu.VMEM((ROWS, COLS), BF16), pltpu.VMEM((ROWS, COLS), BF16),
            pltpu.VMEM((2 * HROWS, 2 * D), F32),
        ],
        compiler_params=pltpu.CompilerParams(vmem_limit_bytes=48 * 2**20),
        name="attend",
    )(starts, imports, lens, q, do, kvwin, slots, far)


def exit_kernel(
    starts_hbm, imports_hbm, dq, dkv_hbm, packed,
    dq_out, dk_out, dv_out,
    starts, imports, dkv, mine, theirs, tab, y1out, y1in, y2out, y2in, acc, tz, rz, wout, win, coll,
    fsem, ysend, yrecv, qsend, qrecv, local, wsend, wrecv, xsend, xrecv, zsend, zrecv,
    hsend, hrecv,
):
    xh, y, z, xl, co = position()
    me = xl * 2 + co
    c = ctx_of(xh, y, z)
    width = HEADS * D
    slots = 2 * IMPORTS
    first = fetch(
        (
            (starts_hbm, starts), (imports_hbm, imports), (dkv_hbm, dkv),
            (packed, mine.at[pl.ds(0, slots)]),
            (dq.at[rows(me * BLK, BLK), :], dq_out.at[:, rows(me * width, width)]),
        ),
        fsem,
    )
    mine[slots] = jnp.zeros((HDR, 2 * D), BF16)
    theirs[slots] = jnp.zeros((HDR, 2 * D), BF16)
    greet(all_peers(xh, y, z, xl, co))
    x_copy = remote(packed, theirs.at[pl.ds(0, slots)], xsend, xrecv, {"ctx_0": 1 - xh})
    x_copy.start()
    first[2].wait()
    back = ctx_shifted(xh, y, z, -1)
    w_copies = [
        remote(wout.at[s], win.at[s], wsend.at[s], wrecv.at[s], back) for s in range(REACH)
    ]
    wout[0] = dkv[0:TOK, :].astype(BF16)
    w_copies[0].start()
    for n in (0, 1, 3):
        first[n].wait()
    offset = own_header_offset(starts, c * TOK)
    places = []
    for shard_at in (c, ctx_of(1 - xh, y, z)):
        _, _, blocks = header_blocks(starts, imports, shard_at)
        places += [blocks[0:IMPORTS], blocks[IMPORTS:]]

    def find(blocks, base, shard):
        at = jnp.int32(slots)
        for m, (used, block) in enumerate(blocks):
            at = jnp.where(used & (block == shard), base + m, at)
        return at

    def collect(buffer, lists, n):
        shard = xh * (NY * NZ) + n
        return (
            buffer[find(lists[0], 0, shard)].astype(F32)
            + buffer[find(lists[1], IMPORTS, shard)].astype(F32)
        )

    def start_dq():
        copies = []
        for d in (2, 3, 1):
            peer, a = head_peer(xl, co, d)
            copies.append(remote(
                dq.at[rows(a * BLK, BLK), :], dq_out.at[:, rows(me * width, width)],
                qsend.at[d - 1], qrecv.at[d - 1], peer,
            ))
            copies[-1].start()
        return copies

    def own_part(n, carry):
        tab[n] = collect(mine, places[0:2], n)
        return carry

    def peer_part(n, carry):
        tab[n] = tab[n] + collect(theirs, places[2:4], n)
        return carry

    lax.fori_loop(0, NY * NZ, own_part, 0)
    x_copy.wait_recv()
    q_copies = start_dq()
    lax.fori_loop(0, NY * NZ, peer_part, 0)
    near, other = y_neighbours(y)
    across = 2 * lax.rem(lax.div(y, 2) + 1, 2) + lax.rem(y, 2)
    y_copies = []
    for n, to in enumerate((near, other)):
        y1out[n] = tab[rows(across * NZ, NZ), :, n * D:(n + 1) * D].astype(BF16)
        y_copies.append(remote(
            y1out.at[n], y1in.at[n], ysend.at[n], yrecv.at[n], {"ctx_1": to}
        ))
        y_copies[-1].start()
    w_copies[0].wait_recv()
    wout[1] = (win[0].astype(F32) + dkv[TOK:2 * TOK, :]).astype(BF16)
    w_copies[1].start()
    for n, to in enumerate((other, near)):
        y_copies[n].wait_recv()
        plane = rows(to * NZ, NZ)
        add = slice(n * D, (n + 1) * D)
        rest = slice((1 - n) * D, (2 - n) * D)
        y2out[n, :, :, add] = (tab[plane, :, add] + y1in[n].astype(F32)).astype(BF16)
        y2out[n, :, :, rest] = tab[plane, :, rest].astype(BF16)
        y_copies.append(remote(
            y2out.at[n], y2in.at[n], ysend.at[2 + n], yrecv.at[2 + n], {"ctx_1": to}
        ))
        y_copies[-1].start()
    w_copies[1].wait_recv()
    wout[2] = (win[1].astype(F32) + dkv[2 * TOK:3 * TOK, :]).astype(BF16)
    w_copies[2].start()
    for copy in y_copies[2:]:
        copy.wait_recv()
    acc[...] = tab[rows(y * NZ, NZ)] + y2in[0].astype(F32) + y2in[1].astype(F32)
    tz[...] = acc[...].astype(BF16)
    z_copies = []
    for d in (4, 3, 5, 2, 6, 1, 7):
        to = lax.rem(z + d, NZ)
        z_copies.append(remote(
            tz.at[to], rz.at[d - 1], zsend.at[d - 1], zrecv.at[d - 1], {"ctx_2": to}
        ))
        z_copies[-1].start()
    w_copies[2].wait_recv()
    wout[3] = (win[2].astype(F32) + dkv[3 * TOK:4 * TOK, :]).astype(BF16)
    w_copies[3].start()
    header = acc[z]
    for copy in z_copies:
        copy.wait_recv()
    for d in range(NZ - 1):
        header = header + rz[d].astype(F32)
    w_copies[3].wait_recv()
    for b in range(QB):
        part = slice(b * BLK, (b + 1) * BLK)
        keep = jnp.where(offset == b * BLK, 1.0, 0.0)
        coll[part, :] = (
            dkv[REACH * TOK + b * BLK:REACH * TOK + (b + 1) * BLK, :]
            + win[REACH - 1, part, :].astype(F32)
            + header * keep
        )
    h_copies = []
    for d in (2, 3, 1):
        peer, a = head_peer(xl, co, d)
        for n, dst in enumerate((dk_out, dv_out)):
            h_copies.append(remote(
                coll.at[rows(a * BLK, BLK), pl.ds(n * D, D)], dst.at[:, rows(me * D, D)],
                hsend.at[d - 1, n], hrecv.at[d - 1, n], peer,
            ))
            h_copies[-1].start()
    for n, dst in enumerate((dk_out, dv_out)):
        dst[:, rows(me * D, D)] = coll[rows(me * BLK, BLK), n * D:(n + 1) * D]
    first[4].wait()
    for copy in q_copies + h_copies:
        copy.wait_recv()
    for copy in y_copies + w_copies + q_copies + [x_copy] + z_copies + h_copies:
        copy.wait_send()


def leave(starts, imports, dq, dkv, packed):
    dma = pltpu.SemaphoreType.DMA
    hbm = pl.BlockSpec(memory_space=pl.ANY)
    vmem = pl.BlockSpec(memory_space=pltpu.VMEM)
    block = (HDR, 2 * D)
    return pl.pallas_call(
        exit_kernel,
        out_shape=(
            jax.ShapeDtypeStruct((BLK, GROUPS * HEADS * D), BF16),
            jax.ShapeDtypeStruct((BLK, GROUPS * D), F32),
            jax.ShapeDtypeStruct((BLK, GROUPS * D), F32),
        ),
        in_specs=[hbm] * 5,
        out_specs=(hbm, vmem, vmem),
        scratch_shapes=[
            pltpu.SMEM(starts.shape, jnp.int32), pltpu.SMEM(imports.shape, jnp.int32),
            pltpu.VMEM(((REACH + 1) * TOK, 2 * D), F32),
            pltpu.VMEM((2 * IMPORTS + 1, *block), BF16), pltpu.VMEM((2 * IMPORTS + 1, *block), BF16),
            pltpu.VMEM((NY * NZ, *block), F32),
            pltpu.VMEM((2, NZ, HDR, D), BF16), pltpu.VMEM((2, NZ, HDR, D), BF16),
            pltpu.VMEM((2, NZ, *block), BF16), pltpu.VMEM((2, NZ, *block), BF16),
            pltpu.VMEM((NZ, *block), F32), pltpu.VMEM((NZ, *block), BF16),
            pltpu.VMEM((NZ - 1, *block), BF16),
            pltpu.VMEM((REACH, TOK, 2 * D), BF16), pltpu.VMEM((REACH, TOK, 2 * D), BF16),
            pltpu.VMEM((TOK, 2 * D), F32),
            dma((5,)), dma((4,)), dma((4,)), dma((3,)), dma((3,)), dma,
            dma((REACH,)), dma((REACH,)), dma, dma, dma((NZ - 1,)), dma((NZ - 1,)),
            dma((3, 2)), dma((3, 2)),
        ],
        compiler_params=pltpu.CompilerParams(
            collective_id=1, has_side_effects=True, vmem_limit_bytes=32 * 2**20
        ),
        name="leave",
    )(starts, imports, dq, dkv, packed)


def per_device(queries, keys, values, output_gradient, file_starts, file_imports, header_lens):
    q, do, kvwin, slots, far = entry(
        file_starts, file_imports, queries, keys, values, output_gradient
    )
    dq, dkv, packed = compute(
        file_starts, file_imports, header_lens, q, do, kvwin, slots, far
    )
    dq_low, dk, dv = leave(file_starts, file_imports, dq, dkv, packed)
    return dq_low.astype(F32), dk, dv


def solution(mesh):
    split = Mesh(mesh.devices.reshape(NX, NY, NZ, 2, 2), AXES)
    placed = P(AXES, None)
    return jax.shard_map(
        per_device,
        mesh=split,
        in_specs=(placed, placed, placed, placed, P(), P(), P()),
        out_specs=(placed, placed, placed),
        check_vma=False,
    )
```

time: 159 us -> 118 us (0.74)
  the two profiles are of different devices: /device:TPU:9 before, /device:TPU:17 now
where the time goes in v2:
time: 118 us
  Pallas kernels  109 us (92%)
  local copies, waits for them, and re-layouts  6.71 us (6%)
  other arithmetic  1.25 us (1%)
    pallas_call x1, Pallas kernels, entry(): pl.pallas_call(entry_kernel, out_shape=(jax.ShapeDtypeStruct((TOK, HEADS...  47.3 us
    pallas_call x1, Pallas kernels, leave(): pl.pallas_call(exit_kernel, out_shape=(jax.ShapeDtypeStruct((BLK, GROUPS...  44.4 us
    pallas_call x1, Pallas kernels, compute(): pl.pallas_call(compute_kernel, out_shape=(jax.ShapeDtypeStruct((TOK, HEAD...  17.4 us
    unnamed x17, local copies, waits for them, and re-layouts  6.71 us

profile of v2, /device:TPU:17, one launch (start us, length us, event | category | flops | bytes accessed | tf_op | source)
XLA Modules:
  0.0 117.8 jit_solution(10900436156437877181)
XLA Ops:
  0.6 0.0 copy-start.5
  0.6 0.0 copy-start.6
  0.7 0.8 copy.12.imports_hbm.imports
  1.4 0.0 copy-start
  1.4 1.1 copy-done
  2.6 0.0 copy-start.1
  2.6 1.1 copy-done.1
  3.7 0.0 copy-start.2
  3.7 0.8 copy-done.2
  4.5 0.0 copy-start.3
  4.5 0.8 copy-done.3
  5.4 0.0 copy-start.4
  5.4 0.7 copy-done.4
  6.0 47.3 %entry.1 = (bf16[256,1536]{1,0:T(8,128)(2,1)S(1)}, bf16[256,1536]{1,0:T(8,128)(2,1)S(1)}, bf16[1280,256]{1,0:T(8,128)(2,1)S(1)}, bf16[32,64,256]{2,1,0:T(8,128)(2,1)S(1)}, bf16[8,64,256]{2,1,0:T(8,128)(2,1)S(1)}) custom-call(s32[33]{0:T(128)S(1)} %copy-done.4, s32[33,4]{1,0:T(8,128)S(1)} %copy.12.imports_hbm.imports, bf16[64,6144]{1,0:T(8,128)(2,1)S(1)} %copy-done, ...), custom_call_target="tpu_custom_call" | custom-call | tf_op jit(solution)/shard_map/entry/pallas_call | solution.py:241
  53.3 0.0 copy-done.5
  53.3 0.0 copy-done.6
  53.4 17.4 %attend.1 = (bf16[256,1536]{1,0:T(8,128)(2,1)S(1)}, f32[1280,256]{1,0:T(8,128)S(1)}, bf16[8,64,256]{2,1,0:T(8,128)(2,1)S(1)}) custom-call(s32[33]{0:T(128)S(1)} %copy-done.5, s32[33,4]{1,0:T(8,128)S(1)} %copy.12.imports_hbm.imports, s32[33]{0:T(128)S(1)} %copy-done.6, bf16[256,1536]{1,0:T(8,128)(2,1)S(1)} %get-tuple-element.14.q, ...), custom_call_target="tpu_custom_call" | custom-call | tf_op jit(solution)/shard_map/attend/pallas_call | solution.py:372
  70.8 44.4 %leave.1 = (bf16[64,6144]{1,0:T(8,128)(2,1)S(1)}, f32[64,512]{1,0:T(8,128)S(1)}, f32[64,512]{1,0:T(8,128)S(1)}) custom-call(s32[33]{0:T(128)S(1)} %copy-done.5, s32[33,4]{1,0:T(8,128)S(1)} %copy.12.imports_hbm.imports, bf16[256,1536]{1,0:T(8,128)(2,1)S(1)} %get-tuple-element.19.dq, f32[1280,256]{1,0:T(8,128)S(1)} %get-tuple-element.20.dkv_hbm, ...), custom_call_target="tpu_custom_call" | custom-call | tf_op jit(solution)/shard_map/leave/pallas_call | solution.py:546
  115.2 1.2 %convert_element_type.3 = f32[64,6144]{1,0:T(8,128)} convert(bf16[64,6144]{1,0:T(8,128)(2,1)S(1)} %get-tuple-element.22) | non-fusion elementwise | flops 393216 | bytes 2359296 | tf_op jit(solution)/shard_map/convert_element_type | solution.py:585
  116.4 0.7 copy.15
  117.1 0.7 copy.16
Async XLA Ops:
  0.6 52.7 %copy-start.5 = (s32[33]{0:T(128)S(1)}, s32[33]{0:T(128)}, u32[]{:S(2)}) copy-start(s32[33]{0:T(128)} %starts_hbm.3) | copy-start | bytes 400
  0.6 52.7 %copy-start.6 = (s32[33]{0:T(128)S(1)}, s32[33]{0:T(128)}, u32[]{:S(2)}) copy-start(s32[33]{0:T(128)} %lens.1) | copy-start | bytes 400
  1.4 1.1 copy-start
  2.6 1.1 copy-start.1
  3.7 0.8 copy-start.2
  4.5 0.8 copy-start.3
  5.4 0.7 copy-start.4

commit v3 on v2

v3 whole, which is shorter than its diff:
```python
import math

import jax
import jax.numpy as jnp
from jax import lax
from jax.experimental import pallas as pl
from jax.experimental.pallas import tpu as pltpu
from jax.sharding import Mesh
from jax.sharding import PartitionSpec as P

WIN = 1024
HDR = 64
TOK = 256
BLK = 64
D = 128
HEADS = 12
GROUPS = 4
REACH = WIN // TOK
QB = TOK // BLK
IMPORTS = 4
FILES = 33
VMEM_LIMIT = 60 * 2**20
NX, NY, NZ = 2, 4, 8
NCTX = NX * NY * NZ
WROWS = WIN + BLK
HROWS = IMPORTS * HDR
ROWS = WROWS + HROWS
CHUNK_HEADS = 4
CHUNKS = HEADS // CHUNK_HEADS
CW = CHUNK_HEADS * BLK
COLS = HEADS * BLK
SCALE = 1.0 / math.sqrt(D)
LOG2E = 1.4426950408889634
HIDDEN = -1e30
MESH = pl.DeviceIdType.MESH
F32 = jnp.float32
BF16 = jnp.bfloat16
AXES = ("ctx_0", "ctx_1", "ctx_2", "head_0", "head_1")


def position():
    return tuple(lax.axis_index(a) for a in AXES)


def ctx_of(xh, y, z):
    return xh * (NY * NZ) + y * NZ + z


def ctx_shifted(xh, y, z, step):
    c = lax.rem(ctx_of(xh, y, z) + (NCTX + step), NCTX)
    return {
        "ctx_0": lax.div(c, NY * NZ),
        "ctx_1": lax.rem(lax.div(c, NZ), NY),
        "ctx_2": lax.rem(c, NZ),
    }


def head_peer(xl, co, d):
    pxl = 1 - xl if d & 2 else xl
    pco = 1 - co if d & 1 else co
    return {"head_0": pxl, "head_1": pco}, pxl * 2 + pco


def greet(peers):
    barrier = pltpu.get_barrier_semaphore()
    for peer in peers:
        pl.semaphore_signal(barrier, inc=1, device_id=peer, device_id_type=MESH)
    pl.semaphore_wait(barrier, len(peers))


def remote(src, dst, send, recv, peer):
    return pltpu.make_async_remote_copy(
        src_ref=src, dst_ref=dst, send_sem=send, recv_sem=recv, device_id=peer, device_id_type=MESH
    )


def all_peers(xh, y, z, xl, co):
    peers = [head_peer(xl, co, d)[0] for d in (1, 2, 3)]
    peers += [{"ctx_2": lax.rem(z + d, NZ)} for d in range(1, NZ)]
    peers += [{"ctx_1": n} for n in y_neighbours(y)]
    peers += [{"ctx_0": 1 - xh}]
    peers += [ctx_shifted(xh, y, z, 1), ctx_shifted(xh, y, z, -1)]
    return peers


def rows(start, size):
    return pl.ds(pl.multiple_of(start, size), size)


def y_neighbours(y):
    near = y + 1 - 2 * lax.rem(y, 2)
    return near, NY - 1 - y


def file_at(starts, place):
    count = jnp.int32(-1)
    for f in range(starts.shape[0]):
        count = count + jnp.where(starts[f] <= place, 1, 0)
    return count


def header_blocks(starts, imports, c):
    lower = file_at(starts, c * TOK)
    upper = file_at(starts, c * TOK + TOK - 1)
    blocks = []
    for file in (lower, upper):
        for m in range(IMPORTS):
            g = imports[m, file]
            blocks.append((g >= 0, lax.div(starts[jnp.maximum(g, 0)], TOK)))
    return lower, upper, blocks


def own_header_offset(starts, base):
    offset = jnp.int32(0)
    for f in range(starts.shape[0]):
        at = starts[f] - base
        offset = offset + jnp.where((at >= 0) & (at < TOK), at, 0)
    return offset


def fetch(pairs, sems):
    copies = [pltpu.make_async_copy(src, dst, sems.at[n]) for n, (src, dst) in enumerate(pairs)]
    for copy in copies:
        copy.start()
    return copies


def fold8(x, op):
    out = x[0:8]
    for r in range(8, x.shape[0], 8):
        out = op(out, x[r:r + 8])
    return out


def rows_at(start, size, multiple):
    return pl.ds(pl.multiple_of(start, multiple), size)


def receive_inputs(q, k, v, do, small, tables, b, sems):
    starts, imports = tables
    xh, y, z, xl, co = position()
    me = xl * 2 + co
    c = ctx_of(xh, y, z)
    width = HEADS * D
    own = REACH * TOK
    kvwin, slots = b["kvwin"], b["slots"]
    here = fetch(
        (
            (k.at[:, rows(me * D, D)], kvwin.at[rows(own + me * BLK, BLK), pl.ds(0, D)]),
            (v.at[:, rows(me * D, D)], kvwin.at[rows(own + me * BLK, BLK), pl.ds(D, D)]),
            (q.at[:, rows(me * width, width)], b["q"].at[rows(me * BLK, BLK), :]),
            (do.at[:, rows(me * width, width)], b["do"].at[rows(me * BLK, BLK), :]),
        ),
        sems["here"],
    )
    greet(all_peers(xh, y, z, xl, co))
    kv_copies, q_copies = [], []
    for d in (2, 3, 1):
        peer, a = head_peer(xl, co, d)
        for n, src in enumerate((k, v)):
            kv_copies.append(remote(
                src.at[:, rows(a * D, D)],
                kvwin.at[rows(own + me * BLK, BLK), pl.ds(n * D, D)],
                sems["hsend"].at[d - 1, n], sems["hrecv"].at[d - 1, n], peer,
            ))
            kv_copies[-1].start()
    for d in (2, 3, 1):
        peer, a = head_peer(xl, co, d)
        for n, (src, dst) in enumerate(((q, b["q"]), (do, b["do"]))):
            q_copies.append(remote(
                src.at[:, rows(a * width, width)], dst.at[rows(me * BLK, BLK), :],
                sems["qsend"].at[d - 1, n], sems["qrecv"].at[d - 1, n], peer,
            ))
            q_copies[-1].start()
    for copy in small:
        copy.wait()
    offset = own_header_offset(starts, c * TOK)
    for copy in here[:2]:
        copy.wait()
    for copy in kv_copies:
        copy.wait_recv()

    forward = ctx_shifted(xh, y, z, 1)
    w_copies = [
        remote(
            kvwin.at[pl.ds((REACH - s) * TOK, TOK), :],
            kvwin.at[pl.ds((REACH - 1 - s) * TOK, TOK), :],
            sems["wsend"].at[s], sems["wrecv"].at[s], forward,
        )
        for s in range(REACH)
    ]
    w_copies[0].start()
    header = jnp.zeros((HDR, 2 * D), F32)
    for n in range(QB):
        keep = jnp.where(offset == n * BLK, 1.0, 0.0)
        header = header + kvwin[own + n * BLK:own + (n + 1) * BLK, :].astype(F32) * keep
    line = y * NZ + z
    slots[line] = header.astype(BF16)
    z_copies = []
    for d in (1, 7, 2, 6, 3, 5, 4):
        z_copies.append(remote(
            slots.at[line], slots.at[line],
            sems["zsend"].at[d - 1], sems["zrecv"].at[d - 1], {"ctx_2": lax.rem(z + d, NZ)},
        ))
        z_copies[-1].start()
    w_copies[0].wait_recv()
    w_copies[1].start()
    for copy in z_copies:
        copy.wait_recv()
    near, other = y_neighbours(y)
    y_copies = []
    for n, to in enumerate((near, other)):
        y_copies.append(remote(
            slots.at[rows(y * NZ, NZ)], slots.at[rows(y * NZ, NZ)],
            sems["ysend"].at[n], sems["yrecv"].at[n], {"ctx_1": to},
        ))
        y_copies[-1].start()
    w_copies[1].wait_recv()
    w_copies[2].start()
    for n, (came, to) in enumerate(((near, other), (other, near))):
        y_copies[n].wait_recv()
        part = slots.at[rows(came * NZ, NZ), :, pl.ds(n * D, D)]
        y_copies.append(
            remote(part, part, sems["ysend"].at[2 + n], sems["yrecv"].at[2 + n], {"ctx_1": to})
        )
        y_copies[-1].start()
    w_copies[2].wait_recv()
    w_copies[3].start()
    _, _, wanted = header_blocks(starts, imports, ctx_of(1 - xh, y, z))
    for copy in y_copies[2:]:
        copy.wait_recv()
    for m, (_, shard) in enumerate(wanted):
        b["picked"][m] = slots[lax.rem(shard, NY * NZ)]
    x_copy = remote(b["picked"], b["far"], sems["xsend"], sems["xrecv"], {"ctx_0": 1 - xh})
    x_copy.start()
    for copy in q_copies:
        copy.wait_recv()
    for copy in here[2:]:
        copy.wait()
    w_copies[3].wait_recv()
    x_copy.wait_recv()
    return kv_copies + q_copies + z_copies + w_copies + y_copies + [x_copy]


def attend_block(qb, starts, imports, lens, b):
    xh, y, z, _, _ = position()
    base = ctx_of(xh, y, z) * TOK
    place = base + qb * BLK
    lower = file_at(starts, base)
    file = file_at(starts, place)
    begin = starts[file]
    kc, vc, bias, s_ref, dp_ref = b["kc"], b["vc"], b["bias"], b["s"], b["dp"]
    p_ref, ds_ref, qs, dos = b["p"].at[qb], b["ds"].at[qb], b["qs"].at[qb], b["dos"].at[qb]
    step = 64
    kc[0:WROWS, :] = b["kvwin"][rows_at(qb * BLK, WROWS, BLK), 0:D]
    vc[0:WROWS, :] = b["kvwin"][rows_at(qb * BLK, WROWS, BLK), D:2 * D]
    key_place = lax.broadcasted_iota(jnp.int32, (WROWS, D), 0) + (place - WIN)
    bias[0:WROWS, :] = jnp.where(key_place >= begin, 0.0, HIDDEN)
    offsets = lax.broadcasted_iota(jnp.int32, (HDR, D), 0)
    for m in range(IMPORTS):
        g = imports[m, file]
        known = jnp.maximum(g, 0)
        length = jnp.where(g >= 0, lens[known], 0)
        here = pl.ds(WROWS + m * HDR, HDR)
        shard = lax.div(starts[known], TOK)
        at = lax.rem(shard, NY * NZ)
        which = jnp.where(file == lower, 0, IMPORTS) + m
        same = jnp.full((HDR, 2 * D), lax.div(shard, NY * NZ)) == xh
        rows_kv = jnp.where(
            same, b["slots"][at].astype(F32), b["far"][which].astype(F32)
        ).astype(BF16)
        kc[here, :] = rows_kv[:, 0:D]
        vc[here, :] = rows_kv[:, D:2 * D]
        bias[here, :] = jnp.where(offsets < length, 0.0, HIDDEN)
    for h in range(HEADS):
        qs[h * BLK:(h + 1) * BLK, :] = b["q"][rows(qb * BLK, BLK), h * D:(h + 1) * D]
        dos[h * BLK:(h + 1) * BLK, :] = b["do"][rows(qb * BLK, BLK), h * D:(h + 1) * D]

    t = lax.broadcasted_iota(jnp.int32, (BLK, CW), 0)
    p_at = lax.broadcasted_iota(jnp.int32, (BLK, CW), 1) % BLK
    nt = (((1,), (1,)), ((), ()))
    for chunk in range(CHUNKS):
        cols = slice(chunk * CW, (chunk + 1) * CW)
        s_ref[...] = lax.dot_general(kc[...], qs[cols, :], nt, preferred_element_type=F32)
        dp_ref[...] = lax.dot_general(vc[...], dos[cols, :], nt, preferred_element_type=F32)
        top = None
        for r in range(0, ROWS, step):
            s = s_ref[r:r + step, :] + jnp.concatenate([bias[r:r + step, :]] * (CW // D), axis=1)
            if r == 0:
                s = jnp.where(t > p_at, s, HIDDEN)
            if r == WIN:
                s = jnp.where(t <= p_at, s, HIDDEN)
            s_ref[r:r + step, :] = s
            part = fold8(s, jnp.maximum)
            top = part if top is None else jnp.maximum(top, part)
        top = jnp.max(top, axis=0, keepdims=True)
        total = jnp.zeros((8, CW), F32)
        centre = jnp.zeros((8, CW), F32)
        for r in range(0, ROWS, step):
            e = jnp.exp2((s_ref[r:r + step, :] - top) * (SCALE * LOG2E))
            s_ref[r:r + step, :] = e
            total = total + fold8(e, jnp.add)
            centre = centre + fold8(e * dp_ref[r:r + step, :], jnp.add)
        inverse = 1.0 / jnp.sum(total, axis=0, keepdims=True)
        centre = jnp.sum(centre, axis=0, keepdims=True) * inverse
        for r in range(0, ROWS, step):
            w = s_ref[r:r + step, :] * inverse
            p_ref[r:r + step, cols] = w.astype(BF16)
            ds_ref[r:r + step, cols] = (w * (dp_ref[r:r + step, :] - centre)).astype(BF16)
    dqt = lax.dot_general(
        kc[...], ds_ref[...], (((0,), (0,)), ((), ())), preferred_element_type=F32
    )
    dq = (dqt.T * SCALE).astype(BF16)
    for h in range(HEADS):
        b["dq"][qb, :, h * D:(h + 1) * D] = dq[h * BLK:(h + 1) * BLK]
    dv = jnp.dot(p_ref[WROWS:, :], dos[...], preferred_element_type=F32)
    dk = jnp.dot(ds_ref[WROWS:, :], qs[...], preferred_element_type=F32) * SCALE
    first = jnp.where(file == lower, 1.0, 0.0)
    for n, share in enumerate((first, 1.0 - first)):
        part = slice(n * HROWS, (n + 1) * HROWS)
        b["hacc"][part, 0:D] += dk * share
        b["hacc"][part, D:2 * D] += dv * share


def fused_kernel(starts_hbm, imports_hbm, lens_hbm, q, k, v, do, dq_out, dk_out, dv_out, *scratch):
    b = dict(zip(BUFFERS, scratch))
    sems = dict(zip(SEMAPHORES, scratch[len(BUFFERS):]))
    starts, imports, lens = b["starts"], b["imports"], b["lens"]
    xh, y, z, xl, co = position()
    me = xl * 2 + co
    c = ctx_of(xh, y, z)
    width = HEADS * D
    slots = 2 * IMPORTS
    dkv, tab, hacc = b["dkv"], b["tab"], b["hacc"]
    mine, theirs = b["mine"], b["theirs"]
    small = fetch(
        ((starts_hbm, starts), (imports_hbm, imports), (lens_hbm, lens)), sems["small"]
    )
    mine[slots] = jnp.zeros((HDR, 2 * D), BF16)
    theirs[slots] = jnp.zeros((HDR, 2 * D), BF16)
    dkv[...] = jnp.zeros_like(dkv)
    hacc[...] = jnp.zeros_like(hacc)
    sent = receive_inputs(q, k, v, do, small, (starts, imports), b, sems)
    offset = own_header_offset(starts, c * TOK)

    def dq_copy(to):
        return remote(
            b["dq"].at[to], dq_out.at[:, rows(me * width, width)],
            sems["dsend"].at[to], sems["drecv"].at[me],
            {"head_0": lax.div(to, 2), "head_1": lax.rem(to, 2)},
        )

    own_dq = pltpu.make_async_copy(
        b["dq"].at[me], dq_out.at[:, rows(me * width, width)], sems["dlocal"]
    )

    def one_block(i, carry):
        turn = jnp.where(i == 3, 0, jnp.where(i == 2, 1, i + 2))
        qb = lax.rem(me + turn, QB)
        attend_block(qb, starts, imports, lens, b)

        @pl.when(i < 3)
        def _():
            dq_copy(qb).start()

        return carry

    lax.fori_loop(0, QB, one_block, 0)
    own_dq.start()
    for m in range(slots):
        mine[m] = hacc[m * HDR:(m + 1) * HDR, :].astype(BF16)
    x_copy = remote(
        mine.at[pl.ds(0, slots)], theirs.at[pl.ds(0, slots)],
        sems["x2send"], sems["x2recv"], {"ctx_0": 1 - xh},
    )
    x_copy.start()

    def window_gradients(qb, carry):
        window = rows_at(qb * BLK, WROWS, BLK)
        dkv[window, 0:D] += jnp.dot(
            b["ds"][qb, 0:WROWS, :], b["qs"][qb], preferred_element_type=F32
        ) * SCALE
        dkv[window, D:2 * D] += jnp.dot(
            b["p"][qb, 0:WROWS, :], b["dos"][qb], preferred_element_type=F32
        )
        return carry

    lax.fori_loop(0, QB, window_gradients, 0)
    back = ctx_shifted(xh, y, z, -1)
    wout, win = b["wout"], b["win"]
    w_copies = [
        remote(wout.at[s], win.at[s], sems["v2send"].at[s], sems["v2recv"].at[s], back)
        for s in range(REACH)
    ]
    wout[0] = dkv[0:TOK, :].astype(BF16)
    w_copies[0].start()

    def pass_on(s):
        w_copies[s - 1].wait_recv()
        wout[s] = (win[s - 1].astype(F32) + dkv[s * TOK:(s + 1) * TOK, :]).astype(BF16)
        w_copies[s].start()

    places = []
    for shard_at in (c, ctx_of(1 - xh, y, z)):
        _, _, blocks = header_blocks(starts, imports, shard_at)
        places += [blocks[0:IMPORTS], blocks[IMPORTS:]]

    def find(blocks, first, shard):
        at = jnp.int32(slots)
        for m, (used, block) in enumerate(blocks):
            at = jnp.where(used & (block == shard), first + m, at)
        return at

    x_copy.wait_recv()

    def one_slot(n, carry):
        shard = xh * (NY * NZ) + n
        total = None
        for buffer, lists in ((mine, places[0:2]), (theirs, places[2:4])):
            for side in range(2):
                part = buffer[find(lists[side], side * IMPORTS, shard)].astype(F32)
                total = part if total is None else total + part
        tab[n] = total
        return carry

    lax.fori_loop(0, NY * NZ, one_slot, 0)
    near, other = y_neighbours(y)
    across = 2 * lax.rem(lax.div(y, 2) + 1, 2) + lax.rem(y, 2)
    y1out, y1in, y2out, y2in = b["y1out"], b["y1in"], b["y2out"], b["y2in"]
    y_copies = []
    for n, to in enumerate((near, other)):
        y1out[n] = tab[rows(across * NZ, NZ), :, n * D:(n + 1) * D].astype(BF16)
        y_copies.append(remote(
            y1out.at[n], y1in.at[n], sems["y2send"].at[n], sems["y2recv"].at[n], {"ctx_1": to}
        ))
        y_copies[-1].start()
    pass_on(1)
    for n, to in enumerate((other, near)):
        y_copies[n].wait_recv()
        plane = rows(to * NZ, NZ)
        add = slice(n * D, (n + 1) * D)
        rest = slice((1 - n) * D, (2 - n) * D)
        y2out[n, :, :, add] = (tab[plane, :, add] + y1in[n].astype(F32)).astype(BF16)
        y2out[n, :, :, rest] = tab[plane, :, rest].astype(BF16)
        y_copies.append(remote(
            y2out.at[n], y2in.at[n], sems["y2send"].at[2 + n], sems["y2recv"].at[2 + n],
            {"ctx_1": to},
        ))
        y_copies[-1].start()
    pass_on(2)
    for copy in y_copies[2:]:
        copy.wait_recv()
    acc, tz, rz, coll = b["acc"], b["tz"], b["rz"], b["coll"]
    acc[...] = tab[rows(y * NZ, NZ)] + y2in[0].astype(F32) + y2in[1].astype(F32)
    tz[...] = acc[...].astype(BF16)
    z_copies = []
    for d in (4, 3, 5, 2, 6, 1, 7):
        to = lax.rem(z + d, NZ)
        z_copies.append(remote(
            tz.at[to], rz.at[d - 1], sems["z2send"].at[d - 1], sems["z2recv"].at[d - 1],
            {"ctx_2": to},
        ))
        z_copies[-1].start()
    pass_on(3)
    header = acc[z]
    for copy in z_copies:
        copy.wait_recv()
    for d in range(NZ - 1):
        header = header + rz[d].astype(F32)
    w_copies[3].wait_recv()
    for n in range(QB):
        part = slice(n * BLK, (n + 1) * BLK)
        keep = jnp.where(offset == n * BLK, 1.0, 0.0)
        coll[part, :] = (
            dkv[REACH * TOK + n * BLK:REACH * TOK + (n + 1) * BLK, :]
            + win[REACH - 1, part, :].astype(F32)
            + header * keep
        )
    h_copies = []
    for d in (2, 3, 1):
        peer, a = head_peer(xl, co, d)
        for n, dst in enumerate((dk_out, dv_out)):
            h_copies.append(remote(
                coll.at[rows(a * BLK, BLK), pl.ds(n * D, D)], dst.at[:, rows(me * D, D)],
                sems["h2send"].at[d - 1, n], sems["h2recv"].at[d - 1, n], peer,
            ))
            h_copies[-1].start()
    for n, dst in enumerate((dk_out, dv_out)):
        dst[:, rows(me * D, D)] = coll[rows(me * BLK, BLK), n * D:(n + 1) * D]
    own_dq.wait()
    for d in (1, 2, 3):
        _, a = head_peer(xl, co, d)
        remote(
            b["dq"].at[a], dq_out.at[:, rows(a * width, width)],
            sems["dsend"].at[a], sems["drecv"].at[a],
            {"head_0": lax.div(a, 2), "head_1": lax.rem(a, 2)},
        ).wait()
    for copy in h_copies:
        copy.wait_recv()
    for copy in sent + y_copies + w_copies + [x_copy] + z_copies + h_copies:
        copy.wait_send()


def memory():
    vmem, smem = pltpu.VMEM, pltpu.SMEM
    dma = pltpu.SemaphoreType.DMA
    block = (HDR, 2 * D)
    buffers = dict(
        starts=smem((FILES,), jnp.int32), imports=smem((IMPORTS, FILES), jnp.int32),
        lens=smem((FILES,), jnp.int32),
        q=vmem((TOK, HEADS * D), BF16), do=vmem((TOK, HEADS * D), BF16),
        kvwin=vmem(((REACH + 1) * TOK, 2 * D), BF16),
        slots=vmem((NY * NZ, *block), BF16),
        picked=vmem((2 * IMPORTS, *block), BF16), far=vmem((2 * IMPORTS, *block), BF16),
        kc=vmem((ROWS, D), BF16), vc=vmem((ROWS, D), BF16), bias=vmem((ROWS, D), F32),
        qs=vmem((QB, COLS, D), BF16), dos=vmem((QB, COLS, D), BF16),
        s=vmem((ROWS, CW), F32), dp=vmem((ROWS, CW), F32),
        p=vmem((QB, ROWS, COLS), BF16), ds=vmem((QB, ROWS, COLS), BF16),
        hacc=vmem((2 * HROWS, 2 * D), F32),
        dq=vmem((QB, BLK, HEADS * D), BF16),
        dkv=vmem(((REACH + 1) * TOK, 2 * D), F32),
        mine=vmem((2 * IMPORTS + 1, *block), BF16), theirs=vmem((2 * IMPORTS + 1, *block), BF16),
        tab=vmem((NY * NZ, *block), F32),
        y1out=vmem((2, NZ, HDR, D), BF16), y1in=vmem((2, NZ, HDR, D), BF16),
        y2out=vmem((2, NZ, *block), BF16), y2in=vmem((2, NZ, *block), BF16),
        acc=vmem((NZ, *block), F32), tz=vmem((NZ, *block), BF16),
        rz=vmem((NZ - 1, *block), BF16),
        wout=vmem((REACH, TOK, 2 * D), BF16), win=vmem((REACH, TOK, 2 * D), BF16),
        coll=vmem((TOK, 2 * D), F32),
    )
    one, four, window, line, pairs = dma, dma((4,)), dma((REACH,)), dma((NZ - 1,)), dma((3, 2))
    semaphores = dict(
        small=dma((3,)), here=four, hsend=pairs, hrecv=pairs, qsend=pairs, qrecv=pairs,
        wsend=window, wrecv=window, zsend=line, zrecv=line, xsend=one, xrecv=one,
        ysend=four, yrecv=four, dsend=four, drecv=four, dlocal=one,
        v2send=window, v2recv=window, z2send=line, z2recv=line, x2send=one, x2recv=one,
        y2send=four, y2recv=four, h2send=pairs, h2recv=pairs,
    )
    return buffers, semaphores


BUFFERS, SEMAPHORES = (tuple(d) for d in memory())


def per_device(queries, keys, values, output_gradient, file_starts, file_imports, header_lens):
    hbm = pl.BlockSpec(memory_space=pl.ANY)
    vmem = pl.BlockSpec(memory_space=pltpu.VMEM)
    buffers, semaphores = memory()
    dq, dk, dv = pl.pallas_call(
        fused_kernel,
        out_shape=(
            jax.ShapeDtypeStruct((BLK, GROUPS * HEADS * D), BF16),
            jax.ShapeDtypeStruct((BLK, GROUPS * D), F32),
            jax.ShapeDtypeStruct((BLK, GROUPS * D), F32),
        ),
        in_specs=[hbm] * 7,
        out_specs=(hbm, vmem, vmem),
        scratch_shapes=[*buffers.values(), *semaphores.values()],
        compiler_params=pltpu.CompilerParams(
            collective_id=0, has_side_effects=True, vmem_limit_bytes=VMEM_LIMIT
        ),
        name="attention_backward",
    )(
        file_starts, file_imports.T, header_lens, queries, keys, values, output_gradient
    )
    return dq.astype(F32), dk, dv


def solution(mesh):
    split = Mesh(mesh.devices.reshape(NX, NY, NZ, 2, 2), AXES)
    placed = P(AXES, None)
    return jax.shard_map(
        per_device,
        mesh=split,
        in_specs=(placed, placed, placed, placed, P(), P(), P()),
        out_specs=(placed, placed, placed),
        check_vma=False,
    )
```

time: 118 us -> 103 us (0.87)
  the two profiles are of different devices: /device:TPU:17 before, /device:TPU:5 now
where the time goes in v3:
time: 103 us
  Pallas kernels  99 us (96%)
  other arithmetic  2.42 us (2%)
  local copies, waits for them, and re-layouts  1.32 us (1%)
    pallas_call x1, Pallas kernels, per_device(): pl.pallas_call(fused_kernel, out_shape=(jax.ShapeDtypeStruct((BLK, GROUPS...  99 us
    convert_element_type x1, other arithmetic, per_device(): return (dq.astype(F32), dk, dv)  2.42 us

profile of v3, /device:TPU:5, one launch (start us, length us, event | category | flops | bytes accessed | tf_op | source)
XLA Modules:
  0.0 103.4 jit_solution(3092032564152286232)
XLA Ops:
  0.6 99.0 %attention_backward.1 = (bf16[64,6144]{1,0:T(8,128)(2,1)}, f32[64,512]{1,0:T(8,128)}, f32[64,512]{1,0:T(8,128)}) custom-call(s32[33]{0:T(128)} %starts_hbm.1, s32[4,33]{1,0:T(4,128)} %bitcast.1, s32[33]{0:T(128)} %lens_hbm.1, bf16[64,6144]{1,0:T(8,128)(2,1)} %q.1, bf16[64,512]{1,0:T(8,128)(2,1)} %k.1, bf16[64,512]{1,0:T(8,128)(2,1)} %v.1, bf16[64,6144]{1,0:T(8,128)(2,1)} %do.1), custom_call_target="tpu_custom_call" | custom-call | tf_op jit(solution)/shard_map/attention_backward/pallas_call | solution.py:549
  99.6 0.0 copy-start.1
  99.6 0.0 copy-start
  99.6 2.4 %convert_element_type.3 = f32[64,6144]{1,0:T(8,128)} convert(bf16[64,6144]{1,0:T(8,128)(2,1)} %get-tuple-element.6) | non-fusion elementwise | flops 393216 | bytes 2359296 | tf_op jit(solution)/shard_map/convert_element_type | solution.py:566
  102.0 0.0 copy-done.1
  102.0 0.7 copy.12
  102.7 0.0 copy-done
  102.7 0.7 copy.13
Async XLA Ops:
  99.6 2.4 %copy-start.1 = (f32[64,512]{1,0:T(8,128)S(1)}, f32[64,512]{1,0:T(8,128)}, u32[]{:S(2)}) copy-start(f32[64,512]{1,0:T(8,128)} %get-tuple-element.13) | copy-start | bytes 393220
  99.6 3.1 %copy-start = (f32[64,512]{1,0:T(8,128)S(1)}, f32[64,512]{1,0:T(8,128)}, u32[]{:S(2)}) copy-start(f32[64,512]{1,0:T(8,128)} %get-tuple-element.14) | copy-start | bytes 393220

commit v4 on v3

--- a/solution.py
+++ b/solution.py
@@ -143,7 +143,7 @@
     c = ctx_of(xh, y, z)
     width = HEADS * D
     own = REACH * TOK
-    kvwin, slots = b["kvwin"], b["slots"]
+    kvwin, slots = b["kvwin"], (b["slots_k"], b["slots_v"])
     here = fetch(
         (
             (k.at[:, rows(me * D, D)], kvwin.at[rows(own + me * BLK, BLK), pl.ds(0, D)]),
@@ -195,51 +195,73 @@
         keep = jnp.where(offset == n * BLK, 1.0, 0.0)
         header = header + kvwin[own + n * BLK:own + (n + 1) * BLK, :].astype(F32) * keep
     line = y * NZ + z
-    slots[line] = header.astype(BF16)
-    z_copies = []
-    for d in (1, 7, 2, 6, 3, 5, 4):
-        z_copies.append(remote(
-            slots.at[line], slots.at[line],
-            sems["zsend"].at[d - 1], sems["zrecv"].at[d - 1], {"ctx_2": lax.rem(z + d, NZ)},
+    for n in range(2):
+        slots[n][line] = header[:, n * D:(n + 1) * D].astype(BF16)
+    z_copies = ([], [])
+    for n in range(2):
+        for d in (1, 7, 2, 6, 3, 5, 4):
+            part = slots[n].at[line]
+            z_copies[n].append(remote(
+                part, part, sems["zsend"].at[n, d - 1], sems["zrecv"].at[n, d - 1],
+                {"ctx_2": lax.rem(z + d, NZ)},
+            ))
+            z_copies[n][-1].start()
+    near, other = y_neighbours(y)
+    near_copies, far_copies, x_copies = ([], []), ([], []), []
+
+    def to_neighbours(n):
+        for copy in z_copies[n]:
+            copy.wait_recv()
+        for d, to in enumerate((near, other)):
+            part = slots[n].at[rows(y * NZ, NZ)]
+            near_copies[n].append(remote(
+                part, part, sems["ysend"].at[n, d], sems["yrecv"].at[n, d], {"ctx_1": to}
+            ))
+            near_copies[n][-1].start()
+
+    def to_opposite(n):
+        for d, (came, to) in enumerate(((near, other), (other, near))):
+            near_copies[n][d].wait_recv()
+            part = slots[n].at[rows(came * NZ + d * (NZ // 2), NZ // 2)]
+            far_copies[n].append(remote(
+                part, part, sems["ysend"].at[n, 2 + d], sems["yrecv"].at[n, 2 + d],
+                {"ctx_1": to},
+            ))
+            far_copies[n][-1].start()
+
+    def to_other_half(n):
+        for copy in far_copies[n]:
+            copy.wait_recv()
+        for m, (_, shard) in enumerate(wanted):
+            b["picked"][n, m] = slots[n][lax.rem(shard, NY * NZ)]
+        x_copies.append(remote(
+            b["picked"].at[n], b["far"].at[n], sems["xsend"].at[n], sems["xrecv"].at[n],
+            {"ctx_0": 1 - xh},
         ))
-        z_copies[-1].start()
+        x_copies[-1].start()
+
+    _, _, wanted = header_blocks(starts, imports, ctx_of(1 - xh, y, z))
+    to_neighbours(0)
     w_copies[0].wait_recv()
     w_copies[1].start()
-    for copy in z_copies:
-        copy.wait_recv()
-    near, other = y_neighbours(y)
-    y_copies = []
-    for n, to in enumerate((near, other)):
-        y_copies.append(remote(
-            slots.at[rows(y * NZ, NZ)], slots.at[rows(y * NZ, NZ)],
-            sems["ysend"].at[n], sems["yrecv"].at[n], {"ctx_1": to},
-        ))
-        y_copies[-1].start()
+    to_neighbours(1)
+    to_opposite(0)
+    to_opposite(1)
     w_copies[1].wait_recv()
     w_copies[2].start()
-    for n, (came, to) in enumerate(((near, other), (other, near))):
-        y_copies[n].wait_recv()
-        part = slots.at[rows(came * NZ, NZ), :, pl.ds(n * D, D)]
-        y_copies.append(
-            remote(part, part, sems["ysend"].at[2 + n], sems["yrecv"].at[2 + n], {"ctx_1": to})
-        )
-        y_copies[-1].start()
+    to_other_half(0)
+    to_other_half(1)
     w_copies[2].wait_recv()
     w_copies[3].start()
-    _, _, wanted = header_blocks(starts, imports, ctx_of(1 - xh, y, z))
-    for copy in y_copies[2:]:
-        copy.wait_recv()
-    for m, (_, shard) in enumerate(wanted):
-        b["picked"][m] = slots[lax.rem(shard, NY * NZ)]
-    x_copy = remote(b["picked"], b["far"], sems["xsend"], sems["xrecv"], {"ctx_0": 1 - xh})
-    x_copy.start()
     for copy in q_copies:
         copy.wait_recv()
     for copy in here[2:]:
         copy.wait()
     w_copies[3].wait_recv()
-    x_copy.wait_recv()
-    return kv_copies + q_copies + z_copies + w_copies + y_copies + [x_copy]
+    for copy in x_copies:
+        copy.wait_recv()
+    y_copies = near_copies[0] + near_copies[1] + far_copies[0] + far_copies[1]
+    return kv_copies + q_copies + z_copies[0] + z_copies[1] + w_copies + y_copies + x_copies
 
 
 def attend_block(qb, starts, imports, lens, b):
@@ -265,12 +287,10 @@
         shard = lax.div(starts[known], TOK)
         at = lax.rem(shard, NY * NZ)
         which = jnp.where(file == lower, 0, IMPORTS) + m
-        same = jnp.full((HDR, 2 * D), lax.div(shard, NY * NZ)) == xh
-        rows_kv = jnp.where(
-            same, b["slots"][at].astype(F32), b["far"][which].astype(F32)
-        ).astype(BF16)
-        kc[here, :] = rows_kv[:, 0:D]
-        vc[here, :] = rows_kv[:, D:2 * D]
+        same = jnp.full((HDR, D), lax.div(shard, NY * NZ)) == xh
+        for n, (dst, slots) in enumerate(((kc, b["slots_k"]), (vc, b["slots_v"]))):
+            near = slots[at].astype(F32)
+            dst[here, :] = jnp.where(same, near, b["far"][n, which].astype(F32)).astype(BF16)
         bias[here, :] = jnp.where(offsets < length, 0.0, HIDDEN)
     for h in range(HEADS):
         qs[h * BLK:(h + 1) * BLK, :] = b["q"][rows(qb * BLK, BLK), h * D:(h + 1) * D]
@@ -332,12 +352,13 @@
     width = HEADS * D
     slots = 2 * IMPORTS
     dkv, tab, hacc = b["dkv"], b["tab"], b["hacc"]
-    mine, theirs = b["mine"], b["theirs"]
+    mine, theirs = b["mine"], (b["theirs_k"], b["theirs_v"])
     small = fetch(
         ((starts_hbm, starts), (imports_hbm, imports), (lens_hbm, lens)), sems["small"]
     )
-    mine[slots] = jnp.zeros((HDR, 2 * D), BF16)
-    theirs[slots] = jnp.zeros((HDR, 2 * D), BF16)
+    for n in range(2):
+        mine[n, slots] = jnp.zeros((HDR, D), BF16)
+        theirs[n][slots] = jnp.zeros((HDR, D), BF16)
     dkv[...] = jnp.zeros_like(dkv)
     hacc[...] = jnp.zeros_like(hacc)
     sent = receive_inputs(q, k, v, do, small, (starts, imports), b, sems)
@@ -367,13 +388,16 @@
 
     lax.fori_loop(0, QB, one_block, 0)
     own_dq.start()
-    for m in range(slots):
-        mine[m] = hacc[m * HDR:(m + 1) * HDR, :].astype(BF16)
-    x_copy = remote(
-        mine.at[pl.ds(0, slots)], theirs.at[pl.ds(0, slots)],
-        sems["x2send"], sems["x2recv"], {"ctx_0": 1 - xh},
-    )
-    x_copy.start()
+    halves = (slice(0, D), slice(D, 2 * D))
+    x_copies = []
+    for n, half in enumerate(halves):
+        for m in range(slots):
+            mine[n, m] = hacc[m * HDR:(m + 1) * HDR, half].astype(BF16)
+        x_copies.append(remote(
+            mine.at[n, pl.ds(0, slots)], theirs[n].at[pl.ds(0, slots)],
+            sems["x2send"].at[n], sems["x2recv"].at[n], {"ctx_0": 1 - xh},
+        ))
+        x_copies[-1].start()
 
     def window_gradients(qb, carry):
         window = rows_at(qb * BLK, WROWS, BLK)
@@ -411,71 +435,91 @@
             at = jnp.where(used & (block == shard), first + m, at)
         return at
 
-    x_copy.wait_recv()
-
-    def one_slot(n, carry):
-        shard = xh * (NY * NZ) + n
-        total = None
-        for buffer, lists in ((mine, places[0:2]), (theirs, places[2:4])):
-            for side in range(2):
-                part = buffer[find(lists[side], side * IMPORTS, shard)].astype(F32)
-                total = part if total is None else total + part
-        tab[n] = total
-        return carry
-
-    lax.fori_loop(0, NY * NZ, one_slot, 0)
     near, other = y_neighbours(y)
     across = 2 * lax.rem(lax.div(y, 2) + 1, 2) + lax.rem(y, 2)
     y1out, y1in, y2out, y2in = b["y1out"], b["y1in"], b["y2out"], b["y2in"]
-    y_copies = []
-    for n, to in enumerate((near, other)):
-        y1out[n] = tab[rows(across * NZ, NZ), :, n * D:(n + 1) * D].astype(BF16)
-        y_copies.append(remote(
-            y1out.at[n], y1in.at[n], sems["y2send"].at[n], sems["y2recv"].at[n], {"ctx_1": to}
-        ))
-        y_copies[-1].start()
+    acc, tz, rz, coll = b["acc"], b["tz"], b["rz"], b["coll"]
+    near_copies, far_copies, z_copies = ([], []), ([], []), ([], [])
+    middle = NZ // 2
+
+    def to_opposite(n):
+        x_copies[n].wait_recv()
+
+        def one_slot(i, carry):
+            shard = xh * (NY * NZ) + i
+            total = None
+            for buffer, lists in ((mine.at[n], places[0:2]), (theirs[n], places[2:4])):
+                for side in range(2):
+                    part = buffer[find(lists[side], side * IMPORTS, shard)].astype(F32)
+                    total = part if total is None else total + part
+            tab[n, i] = total
+            return carry
+
+        lax.fori_loop(0, NY * NZ, one_slot, 0)
+        for d, to in enumerate((near, other)):
+            y1out[n, d] = tab[n, rows(across * NZ + d * middle, middle)].astype(BF16)
+            far_copies[n].append(remote(
+                y1out.at[n, d], y1in.at[n, d],
+                sems["y2send"].at[n, d], sems["y2recv"].at[n, d], {"ctx_1": to},
+            ))
+            far_copies[n][-1].start()
+
+    def to_neighbours(n):
+        for d, to in enumerate((other, near)):
+            far_copies[n][d].wait_recv()
+            add, rest = d * middle, (1 - d) * middle
+            y2out[n, d, pl.ds(add, middle)] = (
+                tab[n, rows(to * NZ + add, middle)] + y1in[n, d].astype(F32)
+            ).astype(BF16)
+            y2out[n, d, pl.ds(rest, middle)] = tab[n, rows(to * NZ + rest, middle)].astype(BF16)
+            near_copies[n].append(remote(
+                y2out.at[n, d], y2in.at[n, d],
+                sems["y2send"].at[n, 2 + d], sems["y2recv"].at[n, 2 + d], {"ctx_1": to},
+            ))
+            near_copies[n][-1].start()
+
+    def to_owners(n):
+        for copy in near_copies[n]:
+            copy.wait_recv()
+        acc[n] = (
+            tab[n, rows(y * NZ, NZ)] + y2in[n, 0].astype(F32) + y2in[n, 1].astype(F32)
+        )
+        tz[n] = acc[n].astype(BF16)
+        for d in (4, 3, 5, 2, 6, 1, 7):
+            to = lax.rem(z + d, NZ)
+            z_copies[n].append(remote(
+                tz.at[n, to], rz.at[n, d - 1],
+                sems["z2send"].at[n, d - 1], sems["z2recv"].at[n, d - 1], {"ctx_2": to},
+            ))
+            z_copies[n][-1].start()
+
+    to_opposite(0)
     pass_on(1)
-    for n, to in enumerate((other, near)):
-        y_copies[n].wait_recv()
-        plane = rows(to * NZ, NZ)
-        add = slice(n * D, (n + 1) * D)
-        rest = slice((1 - n) * D, (2 - n) * D)
-        y2out[n, :, :, add] = (tab[plane, :, add] + y1in[n].astype(F32)).astype(BF16)
-        y2out[n, :, :, rest] = tab[plane, :, rest].astype(BF16)
-        y_copies.append(remote(
-            y2out.at[n], y2in.at[n], sems["y2send"].at[2 + n], sems["y2recv"].at[2 + n],
-            {"ctx_1": to},
-        ))
-        y_copies[-1].start()
+    to_opposite(1)
+    to_neighbours(0)
     pass_on(2)
-    for copy in y_copies[2:]:
-        copy.wait_recv()
-    acc, tz, rz, coll = b["acc"], b["tz"], b["rz"], b["coll"]
-    acc[...] = tab[rows(y * NZ, NZ)] + y2in[0].astype(F32) + y2in[1].astype(F32)
-    tz[...] = acc[...].astype(BF16)
-    z_copies = []
-    for d in (4, 3, 5, 2, 6, 1, 7):
-        to = lax.rem(z + d, NZ)
-        z_copies.append(remote(
-            tz.at[to], rz.at[d - 1], sems["z2send"].at[d - 1], sems["z2recv"].at[d - 1],
-            {"ctx_2": to},
-        ))
-        z_copies[-1].start()
+    to_neighbours(1)
+    to_owners(0)
     pass_on(3)
-    header = acc[z]
-    for copy in z_copies:
-        copy.wait_recv()
-    for d in range(NZ - 1):
-        header = header + rz[d].astype(F32)
+    to_owners(1)
+    headers = []
+    for n in range(2):
+        header = acc[n, z]
+        for copy in z_copies[n]:
+            copy.wait_recv()
+        for d in range(NZ - 1):
+            header = header + rz[n, d].astype(F32)
+        headers.append(header)
     w_copies[3].wait_recv()
     for n in range(QB):
         part = slice(n * BLK, (n + 1) * BLK)
         keep = jnp.where(offset == n * BLK, 1.0, 0.0)
-        coll[part, :] = (
-            dkv[REACH * TOK + n * BLK:REACH * TOK + (n + 1) * BLK, :]
-            + win[REACH - 1, part, :].astype(F32)
-            + header * keep
-        )
+        for half, header in zip(halves, headers):
+            coll[part, half] = (
+                dkv[REACH * TOK + n * BLK:REACH * TOK + (n + 1) * BLK, half]
+                + win[REACH - 1, part, half].astype(F32)
+                + header * keep
+            )
     h_copies = []
     for d in (2, 3, 1):
         peer, a = head_peer(xl, co, d)
@@ -497,21 +541,23 @@
         ).wait()
     for copy in h_copies:
         copy.wait_recv()
-    for copy in sent + y_copies + w_copies + [x_copy] + z_copies + h_copies:
+    for pair in (near_copies, far_copies, z_copies):
+        sent = sent + pair[0] + pair[1]
+    for copy in sent + w_copies + x_copies + h_copies:
         copy.wait_send()
 
 
 def memory():
     vmem, smem = pltpu.VMEM, pltpu.SMEM
     dma = pltpu.SemaphoreType.DMA
-    block = (HDR, 2 * D)
+    half = (HDR, D)
     buffers = dict(
         starts=smem((FILES,), jnp.int32), imports=smem((IMPORTS, FILES), jnp.int32),
         lens=smem((FILES,), jnp.int32),
         q=vmem((TOK, HEADS * D), BF16), do=vmem((TOK, HEADS * D), BF16),
         kvwin=vmem(((REACH + 1) * TOK, 2 * D), BF16),
-        slots=vmem((NY * NZ, *block), BF16),
-        picked=vmem((2 * IMPORTS, *block), BF16), far=vmem((2 * IMPORTS, *block), BF16),
+        slots_k=vmem((NY * NZ, *half), BF16), slots_v=vmem((NY * NZ, *half), BF16),
+        picked=vmem((2, 2 * IMPORTS, HDR, D), BF16), far=vmem((2, 2 * IMPORTS, HDR, D), BF16),
         kc=vmem((ROWS, D), BF16), vc=vmem((ROWS, D), BF16), bias=vmem((ROWS, D), F32),
         qs=vmem((QB, COLS, D), BF16), dos=vmem((QB, COLS, D), BF16),
         s=vmem((ROWS, CW), F32), dp=vmem((ROWS, CW), F32),
@@ -519,22 +565,25 @@
         hacc=vmem((2 * HROWS, 2 * D), F32),
         dq=vmem((QB, BLK, HEADS * D), BF16),
         dkv=vmem(((REACH + 1) * TOK, 2 * D), F32),
-        mine=vmem((2 * IMPORTS + 1, *block), BF16), theirs=vmem((2 * IMPORTS + 1, *block), BF16),
-        tab=vmem((NY * NZ, *block), F32),
-        y1out=vmem((2, NZ, HDR, D), BF16), y1in=vmem((2, NZ, HDR, D), BF16),
-        y2out=vmem((2, NZ, *block), BF16), y2in=vmem((2, NZ, *block), BF16),
-        acc=vmem((NZ, *block), F32), tz=vmem((NZ, *block), BF16),
-        rz=vmem((NZ - 1, *block), BF16),
+        mine=vmem((2, 2 * IMPORTS + 1, *half), BF16),
+        theirs_k=vmem((2 * IMPORTS + 1, *half), BF16),
+        theirs_v=vmem((2 * IMPORTS + 1, *half), BF16),
+        tab=vmem((2, NY * NZ, *half), F32),
+        y1out=vmem((2, 2, NZ // 2, *half), BF16), y1in=vmem((2, 2, NZ // 2, *half), BF16),
+        y2out=vmem((2, 2, NZ, *half), BF16), y2in=vmem((2, 2, NZ, *half), BF16),
+        acc=vmem((2, NZ, *half), F32), tz=vmem((2, NZ, *half), BF16),
+        rz=vmem((2, NZ - 1, *half), BF16),
         wout=vmem((REACH, TOK, 2 * D), BF16), win=vmem((REACH, TOK, 2 * D), BF16),
         coll=vmem((TOK, 2 * D), F32),
     )
-    one, four, window, line, pairs = dma, dma((4,)), dma((REACH,)), dma((NZ - 1,)), dma((3, 2))
+    four, window, line, pairs = dma((4,)), dma((REACH,)), dma((2, NZ - 1)), dma((3, 2))
+    two, steps = dma((2,)), dma((2, 4))
     semaphores = dict(
         small=dma((3,)), here=four, hsend=pairs, hrecv=pairs, qsend=pairs, qrecv=pairs,
-        wsend=window, wrecv=window, zsend=line, zrecv=line, xsend=one, xrecv=one,
-        ysend=four, yrecv=four, dsend=four, drecv=four, dlocal=one,
-        v2send=window, v2recv=window, z2send=line, z2recv=line, x2send=one, x2recv=one,
-        y2send=four, y2recv=four, h2send=pairs, h2recv=pairs,
+        wsend=window, wrecv=window, zsend=line, zrecv=line, xsend=two, xrecv=two,
+        ysend=steps, yrecv=steps, dsend=four, drecv=four, dlocal=dma,
+        v2send=window, v2recv=window, z2send=line, z2recv=line, x2send=two, x2recv=two,
+        y2send=steps, y2recv=steps, h2send=pairs, h2recv=pairs,
     )
     return buffers, semaphores
 

time: 103 us -> 101 us (0.981)
  the two profiles are of different devices: /device:TPU:5 before, /device:TPU:1 now
where the time goes in v4:
time: 101 us; the launch traced here: 99.7 us
  Pallas kernels  95.3 us (94%)
  other arithmetic  2.42 us (2%)
  local copies, waits for them, and re-layouts  1.32 us (1%)
    pallas_call x1, Pallas kernels, per_device(): pl.pallas_call(fused_kernel, out_shape=(jax.ShapeDtypeStruct((BLK, GROUPS...  95.3 us
    convert_element_type x1, other arithmetic, per_device(): return (dq.astype(F32), dk, dv)  2.42 us

profile of v4, /device:TPU:1, one launch (start us, length us, event | category | flops | bytes accessed | tf_op | source)
XLA Modules:
  0.0 99.7 jit_solution(5380147382057390406)
XLA Ops:
  0.6 95.3 %attention_backward.1 = (bf16[64,6144]{1,0:T(8,128)(2,1)}, f32[64,512]{1,0:T(8,128)}, f32[64,512]{1,0:T(8,128)}) custom-call(s32[33]{0:T(128)} %starts_hbm.1, s32[4,33]{1,0:T(4,128)} %bitcast.1, s32[33]{0:T(128)} %lens_hbm.1, bf16[64,6144]{1,0:T(8,128)(2,1)} %q.1, bf16[64,512]{1,0:T(8,128)(2,1)} %k.1, bf16[64,512]{1,0:T(8,128)(2,1)} %v.1, bf16[64,6144]{1,0:T(8,128)(2,1)} %do.1), custom_call_target="tpu_custom_call" | custom-call | tf_op jit(solution)/shard_map/attention_backward/pallas_call | solution.py:598
  95.9 0.0 copy-start.1
  95.9 0.0 copy-start
  95.9 2.4 %convert_element_type.3 = f32[64,6144]{1,0:T(8,128)} convert(bf16[64,6144]{1,0:T(8,128)(2,1)} %get-tuple-element.6) | non-fusion elementwise | flops 393216 | bytes 2359296 | tf_op jit(solution)/shard_map/convert_element_type | solution.py:615
  98.4 0.0 copy-done.1
  98.4 0.7 copy.12
  99.0 0.0 copy-done
  99.0 0.7 copy.13
Async XLA Ops:
  95.9 2.4 %copy-start.1 = (f32[64,512]{1,0:T(8,128)S(1)}, f32[64,512]{1,0:T(8,128)}, u32[]{:S(2)}) copy-start(f32[64,512]{1,0:T(8,128)} %get-tuple-element.13) | copy-start | bytes 393220
  95.9 3.1 %copy-start = (f32[64,512]{1,0:T(8,128)S(1)}, f32[64,512]{1,0:T(8,128)}, u32[]{:S(2)}) copy-start(f32[64,512]{1,0:T(8,128)} %get-tuple-element.14) | copy-start | bytes 393220

commit v5 on v4

--- a/solution.py
+++ b/solution.py
@@ -271,8 +271,9 @@
     lower = file_at(starts, base)
     file = file_at(starts, place)
     begin = starts[file]
-    kc, vc, bias, s_ref, dp_ref = b["kc"], b["vc"], b["bias"], b["s"], b["dp"]
-    p_ref, ds_ref, qs, dos = b["p"].at[qb], b["ds"].at[qb], b["qs"].at[qb], b["dos"].at[qb]
+    kc, vc, bias = b["kc"].at[qb], b["vc"], b["bias"]
+    qs, dos = b["qs"].at[qb], b["dos"].at[qb]
+    p_ref, ds_ref = b["hp"], b["hds"].at[qb]
     step = 64
     kc[0:WROWS, :] = b["kvwin"][rows_at(qb * BLK, WROWS, BLK), 0:D]
     vc[0:WROWS, :] = b["kvwin"][rows_at(qb * BLK, WROWS, BLK), D:2 * D]
@@ -301,6 +302,7 @@
     nt = (((1,), (1,)), ((), ()))
     for chunk in range(CHUNKS):
         cols = slice(chunk * CW, (chunk + 1) * CW)
+        s_ref, dp_ref = b["s"].at[qb, chunk], b["dp"].at[qb, chunk]
         s_ref[...] = lax.dot_general(kc[...], qs[cols, :], nt, preferred_element_type=F32)
         dp_ref[...] = lax.dot_general(vc[...], dos[cols, :], nt, preferred_element_type=F32)
         top = None
@@ -323,23 +325,44 @@
             centre = centre + fold8(e * dp_ref[r:r + step, :], jnp.add)
         inverse = 1.0 / jnp.sum(total, axis=0, keepdims=True)
         centre = jnp.sum(centre, axis=0, keepdims=True) * inverse
-        for r in range(0, ROWS, step):
+        b["stat"][qb, chunk, 0:1, :] = inverse
+        b["stat"][qb, chunk, 1:2, :] = centre
+        for r in range(WROWS, ROWS, step):
             w = s_ref[r:r + step, :] * inverse
-            p_ref[r:r + step, cols] = w.astype(BF16)
-            ds_ref[r:r + step, cols] = (w * (dp_ref[r:r + step, :] - centre)).astype(BF16)
-    dqt = lax.dot_general(
-        kc[...], ds_ref[...], (((0,), (0,)), ((), ())), preferred_element_type=F32
-    )
-    dq = (dqt.T * SCALE).astype(BF16)
-    for h in range(HEADS):
-        b["dq"][qb, :, h * D:(h + 1) * D] = dq[h * BLK:(h + 1) * BLK]
-    dv = jnp.dot(p_ref[WROWS:, :], dos[...], preferred_element_type=F32)
-    dk = jnp.dot(ds_ref[WROWS:, :], qs[...], preferred_element_type=F32) * SCALE
+            here = slice(r - WROWS, r - WROWS + step)
+            p_ref[here, cols] = w.astype(BF16)
+            ds_ref[here, cols] = (w * (dp_ref[r:r + step, :] - centre)).astype(BF16)
+    dv = jnp.dot(p_ref[...], dos[...], preferred_element_type=F32)
+    dk = jnp.dot(ds_ref[...], qs[...], preferred_element_type=F32) * SCALE
     first = jnp.where(file == lower, 1.0, 0.0)
     for n, share in enumerate((first, 1.0 - first)):
         part = slice(n * HROWS, (n + 1) * HROWS)
         b["hacc"][part, 0:D] += dk * share
         b["hacc"][part, D:2 * D] += dv * share
+
+
+def window_block(qb, b):
+    kc, p_ref, ds_ref, hds = b["kc"].at[qb], b["p"], b["ds"], b["hds"].at[qb]
+    step = 64
+    for chunk in range(CHUNKS):
+        cols = slice(chunk * CW, (chunk + 1) * CW)
+        s_ref, dp_ref = b["s"].at[qb, chunk], b["dp"].at[qb, chunk]
+        inverse = b["stat"][qb, chunk, 0:1, :]
+        centre = b["stat"][qb, chunk, 1:2, :]
+        for r in range(0, WROWS, step):
+            w = s_ref[r:r + step, :] * inverse
+            p_ref[r:r + step, cols] = w.astype(BF16)
+            ds_ref[r:r + step, cols] = (w * (dp_ref[r:r + step, :] - centre)).astype(BF16)
+    tn = (((0,), (0,)), ((), ()))
+    dqt = lax.dot_general(kc[0:WROWS, :], ds_ref[...], tn, preferred_element_type=F32)
+    dqt = dqt + lax.dot_general(kc[WROWS:, :], hds[...], tn, preferred_element_type=F32)
+    dq = (dqt.T * SCALE).astype(BF16)
+    for h in range(HEADS):
+        b["dq"][qb, :, h * D:(h + 1) * D] = dq[h * BLK:(h + 1) * BLK]
+    window = rows_at(qb * BLK, WROWS, BLK)
+    dkv = b["dkv"]
+    dkv[window, 0:D] += jnp.dot(ds_ref[...], b["qs"][qb], preferred_element_type=F32) * SCALE
+    dkv[window, D:2 * D] += jnp.dot(p_ref[...], b["dos"][qb], preferred_element_type=F32)
 
 
 def fused_kernel(starts_hbm, imports_hbm, lens_hbm, q, k, v, do, dq_out, dk_out, dv_out, *scratch):
@@ -375,10 +398,17 @@
         b["dq"].at[me], dq_out.at[:, rows(me * width, width)], sems["dlocal"]
     )
 
-    def one_block(i, carry):
+    def block_of(i):
         turn = jnp.where(i == 3, 0, jnp.where(i == 2, 1, i + 2))
-        qb = lax.rem(me + turn, QB)
-        attend_block(qb, starts, imports, lens, b)
+        return lax.rem(me + turn, QB)
+
+    def first_half(i, carry):
+        attend_block(i, starts, imports, lens, b)
+        return carry
+
+    def second_half(i, carry):
+        qb = block_of(i)
+        window_block(qb, b)
 
         @pl.when(i < 3)
         def _():
@@ -386,8 +416,7 @@
 
         return carry
 
-    lax.fori_loop(0, QB, one_block, 0)
-    own_dq.start()
+    lax.fori_loop(0, QB, first_half, 0)
     halves = (slice(0, D), slice(D, 2 * D))
     x_copies = []
     for n, half in enumerate(halves):
@@ -399,25 +428,12 @@
         ))
         x_copies[-1].start()
 
-    def window_gradients(qb, carry):
-        window = rows_at(qb * BLK, WROWS, BLK)
-        dkv[window, 0:D] += jnp.dot(
-            b["ds"][qb, 0:WROWS, :], b["qs"][qb], preferred_element_type=F32
-        ) * SCALE
-        dkv[window, D:2 * D] += jnp.dot(
-            b["p"][qb, 0:WROWS, :], b["dos"][qb], preferred_element_type=F32
-        )
-        return carry
-
-    lax.fori_loop(0, QB, window_gradients, 0)
     back = ctx_shifted(xh, y, z, -1)
     wout, win = b["wout"], b["win"]
     w_copies = [
         remote(wout.at[s], win.at[s], sems["v2send"].at[s], sems["v2recv"].at[s], back)
         for s in range(REACH)
     ]
-    wout[0] = dkv[0:TOK, :].astype(BF16)
-    w_copies[0].start()
 
     def pass_on(s):
         w_copies[s - 1].wait_recv()
@@ -493,15 +509,19 @@
             ))
             z_copies[n][-1].start()
 
+    lax.fori_loop(0, QB, second_half, 0)
+    own_dq.start()
+    wout[0] = dkv[0:TOK, :].astype(BF16)
+    w_copies[0].start()
     to_opposite(0)
-    pass_on(1)
     to_opposite(1)
     to_neighbours(0)
-    pass_on(2)
+    pass_on(1)
     to_neighbours(1)
     to_owners(0)
+    pass_on(2)
+    to_owners(1)
     pass_on(3)
-    to_owners(1)
     headers = []
     for n in range(2):
         header = acc[n, z]
@@ -558,10 +578,12 @@
         kvwin=vmem(((REACH + 1) * TOK, 2 * D), BF16),
         slots_k=vmem((NY * NZ, *half), BF16), slots_v=vmem((NY * NZ, *half), BF16),
         picked=vmem((2, 2 * IMPORTS, HDR, D), BF16), far=vmem((2, 2 * IMPORTS, HDR, D), BF16),
-        kc=vmem((ROWS, D), BF16), vc=vmem((ROWS, D), BF16), bias=vmem((ROWS, D), F32),
+        kc=vmem((QB, ROWS, D), BF16), vc=vmem((ROWS, D), BF16), bias=vmem((ROWS, D), F32),
         qs=vmem((QB, COLS, D), BF16), dos=vmem((QB, COLS, D), BF16),
-        s=vmem((ROWS, CW), F32), dp=vmem((ROWS, CW), F32),
-        p=vmem((QB, ROWS, COLS), BF16), ds=vmem((QB, ROWS, COLS), BF16),
+        s=vmem((QB, CHUNKS, ROWS, CW), F32), dp=vmem((QB, CHUNKS, ROWS, CW), F32),
+        stat=vmem((QB, CHUNKS, 8, CW), F32),
+        p=vmem((WROWS, COLS), BF16), ds=vmem((WROWS, COLS), BF16),
+        hp=vmem((HROWS, COLS), BF16), hds=vmem((QB, HROWS, COLS), BF16),
         hacc=vmem((2 * HROWS, 2 * D), F32),
         dq=vmem((QB, BLK, HEADS * D), BF16),
         dkv=vmem(((REACH + 1) * TOK, 2 * D), F32),

time: 101 us -> 94.2 us (0.933)
  Pallas kernels: 95.3 us -> 88.2 us
    pallas_call x1, Pallas kernels: 95.3 us -> 88.2 us  [per_device(): pl.pallas_call(fused_kernel, out_shape=(jax.ShapeDtypeStruct((BLK, GROUPS...]
where the time goes in v5:
time: 94.2 us; the launch traced here: 92.5 us
  Pallas kernels  88.2 us (94%)
  other arithmetic  2.42 us (3%)
  local copies, waits for them, and re-layouts  1.32 us (1%)
    pallas_call x1, Pallas kernels, per_device(): pl.pallas_call(fused_kernel, out_shape=(jax.ShapeDtypeStruct((BLK, GROUPS...  88.2 us
    convert_element_type x1, other arithmetic, per_device(): return (dq.astype(F32), dk, dv)  2.42 us

profile of v5, /device:TPU:1, one launch (start us, length us, event | category | flops | bytes accessed | tf_op | source)
XLA Modules:
  0.0 92.5 jit_solution(897157932756591835)
XLA Ops:
  0.6 88.2 %attention_backward.1 = (bf16[64,6144]{1,0:T(8,128)(2,1)}, f32[64,512]{1,0:T(8,128)}, f32[64,512]{1,0:T(8,128)}) custom-call(s32[33]{0:T(128)} %starts_hbm.1, s32[4,33]{1,0:T(4,128)} %bitcast.1, s32[33]{0:T(128)} %lens_hbm.1, bf16[64,6144]{1,0:T(8,128)(2,1)} %q.1, bf16[64,512]{1,0:T(8,128)(2,1)} %k.1, bf16[64,512]{1,0:T(8,128)(2,1)} %v.1, bf16[64,6144]{1,0:T(8,128)(2,1)} %do.1), custom_call_target="tpu_custom_call" | custom-call | tf_op jit(solution)/shard_map/attention_backward/pallas_call | solution.py:620
  88.8 0.0 copy-start.1
  88.8 0.0 copy-start
  88.8 2.4 %convert_element_type.3 = f32[64,6144]{1,0:T(8,128)} convert(bf16[64,6144]{1,0:T(8,128)(2,1)} %get-tuple-element.6) | non-fusion elementwise | flops 393216 | bytes 2359296 | tf_op jit(solution)/shard_map/convert_element_type | solution.py:637
  91.2 0.0 copy-done.1
  91.2 0.7 copy.12
  91.9 0.0 copy-done
  91.9 0.7 copy.13
Async XLA Ops:
  88.8 2.4 %copy-start.1 = (f32[64,512]{1,0:T(8,128)S(1)}, f32[64,512]{1,0:T(8,128)}, u32[]{:S(2)}) copy-start(f32[64,512]{1,0:T(8,128)} %get-tuple-element.13) | copy-start | bytes 393220
  88.8 3.1 %copy-start = (f32[64,512]{1,0:T(8,128)S(1)}, f32[64,512]{1,0:T(8,128)}, u32[]{:S(2)}) copy-start(f32[64,512]{1,0:T(8,128)} %get-tuple-element.14) | copy-start | bytes 393220

commit v6 on v5

--- a/solution.py
+++ b/solution.py
@@ -342,7 +342,7 @@
 
 
 def window_block(qb, b):
-    kc, p_ref, ds_ref, hds = b["kc"].at[qb], b["p"], b["ds"], b["hds"].at[qb]
+    p_ref, ds_ref = b["p"], b["ds"].at[qb]
     step = 64
     for chunk in range(CHUNKS):
         cols = slice(chunk * CW, (chunk + 1) * CW)
@@ -353,16 +353,20 @@
             w = s_ref[r:r + step, :] * inverse
             p_ref[r:r + step, cols] = w.astype(BF16)
             ds_ref[r:r + step, cols] = (w * (dp_ref[r:r + step, :] - centre)).astype(BF16)
+    window = rows_at(qb * BLK, WROWS, BLK)
+    dkv = b["dkv"]
+    dkv[window, 0:D] += jnp.dot(ds_ref[...], b["qs"][qb], preferred_element_type=F32) * SCALE
+    dkv[window, D:2 * D] += jnp.dot(p_ref[...], b["dos"][qb], preferred_element_type=F32)
+
+
+def query_block(qb, b):
+    kc, ds_ref, hds = b["kc"].at[qb], b["ds"].at[qb], b["hds"].at[qb]
     tn = (((0,), (0,)), ((), ()))
     dqt = lax.dot_general(kc[0:WROWS, :], ds_ref[...], tn, preferred_element_type=F32)
     dqt = dqt + lax.dot_general(kc[WROWS:, :], hds[...], tn, preferred_element_type=F32)
     dq = (dqt.T * SCALE).astype(BF16)
     for h in range(HEADS):
         b["dq"][qb, :, h * D:(h + 1) * D] = dq[h * BLK:(h + 1) * BLK]
-    window = rows_at(qb * BLK, WROWS, BLK)
-    dkv = b["dkv"]
-    dkv[window, 0:D] += jnp.dot(ds_ref[...], b["qs"][qb], preferred_element_type=F32) * SCALE
-    dkv[window, D:2 * D] += jnp.dot(p_ref[...], b["dos"][qb], preferred_element_type=F32)
 
 
 def fused_kernel(starts_hbm, imports_hbm, lens_hbm, q, k, v, do, dq_out, dk_out, dv_out, *scratch):
@@ -407,8 +411,12 @@
         return carry
 
     def second_half(i, carry):
+        window_block(i, b)
+        return carry
+
+    def third_part(i, carry):
         qb = block_of(i)
-        window_block(qb, b)
+        query_block(qb, b)
 
         @pl.when(i < 3)
         def _():
@@ -510,14 +518,16 @@
             z_copies[n][-1].start()
 
     lax.fori_loop(0, QB, second_half, 0)
-    own_dq.start()
     wout[0] = dkv[0:TOK, :].astype(BF16)
     w_copies[0].start()
     to_opposite(0)
     to_opposite(1)
+    lax.fori_loop(0, QB // 2, third_part, 0)
     to_neighbours(0)
     pass_on(1)
     to_neighbours(1)
+    lax.fori_loop(QB // 2, QB, third_part, 0)
+    own_dq.start()
     to_owners(0)
     pass_on(2)
     to_owners(1)
@@ -582,7 +592,7 @@
         qs=vmem((QB, COLS, D), BF16), dos=vmem((QB, COLS, D), BF16),
         s=vmem((QB, CHUNKS, ROWS, CW), F32), dp=vmem((QB, CHUNKS, ROWS, CW), F32),
         stat=vmem((QB, CHUNKS, 8, CW), F32),
-        p=vmem((WROWS, COLS), BF16), ds=vmem((WROWS, COLS), BF16),
+        p=vmem((WROWS, COLS), BF16), ds=vmem((QB, WROWS, COLS), BF16),
         hp=vmem((HROWS, COLS), BF16), hds=vmem((QB, HROWS, COLS), BF16),
         hacc=vmem((2 * HROWS, 2 * D), F32),
         dq=vmem((QB, BLK, HEADS * D), BF16),

time: 94.2 us -> 93.3 us (level)
  no operation moved by 1% of the time
where the time goes in v6:
time: 93.3 us; the launch traced here: 92.1 us
  Pallas kernels  87.7 us (94%)
  other arithmetic  2.42 us (3%)
  local copies, waits for them, and re-layouts  1.32 us (1%)
    pallas_call x1, Pallas kernels, per_device(): pl.pallas_call(fused_kernel, out_shape=(jax.ShapeDtypeStruct((BLK, GROUPS...  87.7 us
    convert_element_type x1, other arithmetic, per_device(): return (dq.astype(F32), dk, dv)  2.42 us

profile of v6, /device:TPU:1, one launch (start us, length us, event | category | flops | bytes accessed | tf_op | source)
XLA Modules:
  0.0 92.1 jit_solution(16161970167773912774)
XLA Ops:
  0.6 87.7 %attention_backward.1 = (bf16[64,6144]{1,0:T(8,128)(2,1)}, f32[64,512]{1,0:T(8,128)}, f32[64,512]{1,0:T(8,128)}) custom-call(s32[33]{0:T(128)} %starts_hbm.1, s32[4,33]{1,0:T(4,128)} %bitcast.1, s32[33]{0:T(128)} %lens_hbm.1, bf16[64,6144]{1,0:T(8,128)(2,1)} %q.1, bf16[64,512]{1,0:T(8,128)(2,1)} %k.1, bf16[64,512]{1,0:T(8,128)(2,1)} %v.1, bf16[64,6144]{1,0:T(8,128)(2,1)} %do.1), custom_call_target="tpu_custom_call" | custom-call | tf_op jit(solution)/shard_map/attention_backward/pallas_call | solution.py:630
  88.4 0.0 copy-start.1
  88.4 0.0 copy-start
  88.4 2.4 %convert_element_type.3 = f32[64,6144]{1,0:T(8,128)} convert(bf16[64,6144]{1,0:T(8,128)(2,1)} %get-tuple-element.6) | non-fusion elementwise | flops 393216 | bytes 2359296 | tf_op jit(solution)/shard_map/convert_element_type | solution.py:647
  90.8 0.0 copy-done.1
  90.8 0.7 copy.12
  91.5 0.0 copy-done
  91.5 0.7 copy.13
Async XLA Ops:
  88.4 2.4 %copy-start.1 = (f32[64,512]{1,0:T(8,128)S(1)}, f32[64,512]{1,0:T(8,128)}, u32[]{:S(2)}) copy-start(f32[64,512]{1,0:T(8,128)} %get-tuple-element.13) | copy-start | bytes 393220
  88.4 3.1 %copy-start = (f32[64,512]{1,0:T(8,128)S(1)}, f32[64,512]{1,0:T(8,128)}, u32[]{:S(2)}) copy-start(f32[64,512]{1,0:T(8,128)} %get-tuple-element.14) | copy-start | bytes 393220

commit v7 on v6

--- a/solution.py
+++ b/solution.py
@@ -531,36 +531,41 @@
     to_owners(0)
     pass_on(2)
     to_owners(1)
-    pass_on(3)
-    headers = []
-    for n in range(2):
+    w_copies[2].wait_recv()
+    last_copies = []
+    for n, half in enumerate(halves):
+        wout[3, :, half] = (
+            win[2, :, half].astype(F32) + dkv[3 * TOK:4 * TOK, half]
+        ).astype(BF16)
+        lanes = pl.ds(n * D, D)
+        last_copies.append(remote(
+            wout.at[3, :, lanes], win.at[3, :, lanes],
+            sems["v2send"].at[3 + n], sems["v2recv"].at[3 + n], back,
+        ))
+        last_copies[-1].start()
+    h_copies = []
+    for n, (half, dst) in enumerate(zip(halves, (dk_out, dv_out))):
         header = acc[n, z]
         for copy in z_copies[n]:
             copy.wait_recv()
         for d in range(NZ - 1):
             header = header + rz[n, d].astype(F32)
-        headers.append(header)
-    w_copies[3].wait_recv()
-    for n in range(QB):
-        part = slice(n * BLK, (n + 1) * BLK)
-        keep = jnp.where(offset == n * BLK, 1.0, 0.0)
-        for half, header in zip(halves, headers):
+        last_copies[n].wait_recv()
+        for block in range(QB):
+            part = slice(block * BLK, (block + 1) * BLK)
+            keep = jnp.where(offset == block * BLK, 1.0, 0.0)
+            at = REACH * TOK + block * BLK
             coll[part, half] = (
-                dkv[REACH * TOK + n * BLK:REACH * TOK + (n + 1) * BLK, half]
-                + win[REACH - 1, part, half].astype(F32)
-                + header * keep
+                dkv[at:at + BLK, half] + win[3, part, half].astype(F32) + header * keep
             )
-    h_copies = []
-    for d in (2, 3, 1):
-        peer, a = head_peer(xl, co, d)
-        for n, dst in enumerate((dk_out, dv_out)):
+        for d in (2, 3, 1):
+            peer, a = head_peer(xl, co, d)
             h_copies.append(remote(
                 coll.at[rows(a * BLK, BLK), pl.ds(n * D, D)], dst.at[:, rows(me * D, D)],
                 sems["h2send"].at[d - 1, n], sems["h2recv"].at[d - 1, n], peer,
             ))
             h_copies[-1].start()
-    for n, dst in enumerate((dk_out, dv_out)):
-        dst[:, rows(me * D, D)] = coll[rows(me * BLK, BLK), n * D:(n + 1) * D]
+        dst[:, rows(me * D, D)] = coll[rows(me * BLK, BLK), half]
     own_dq.wait()
     for d in (1, 2, 3):
         _, a = head_peer(xl, co, d)
@@ -573,7 +578,7 @@
         copy.wait_recv()
     for pair in (near_copies, far_copies, z_copies):
         sent = sent + pair[0] + pair[1]
-    for copy in sent + w_copies + x_copies + h_copies:
+    for copy in sent + w_copies[:3] + last_copies + x_copies + h_copies:
         copy.wait_send()
 
 
@@ -614,7 +619,7 @@
         small=dma((3,)), here=four, hsend=pairs, hrecv=pairs, qsend=pairs, qrecv=pairs,
         wsend=window, wrecv=window, zsend=line, zrecv=line, xsend=two, xrecv=two,
         ysend=steps, yrecv=steps, dsend=four, drecv=four, dlocal=dma,
-        v2send=window, v2recv=window, z2send=line, z2recv=line, x2send=two, x2recv=two,
+        v2send=dma((REACH + 1,)), v2recv=dma((REACH + 1,)), z2send=line, z2recv=line, x2send=two, x2recv=two,
         y2send=steps, y2recv=steps, h2send=pairs, h2recv=pairs,
     )
     return buffers, semaphores

time: 93.3 us -> 92.6 us (level)
  no operation moved by 1% of the time
where the time goes in v7:
time: 92.6 us; the launch traced here: 91.4 us
  Pallas kernels  87 us (94%)
  other arithmetic  2.42 us (3%)
  local copies, waits for them, and re-layouts  1.32 us (1%)
    pallas_call x1, Pallas kernels, per_device(): pl.pallas_call(fused_kernel, out_shape=(jax.ShapeDtypeStruct((BLK, GROUPS...  87 us
    convert_element_type x1, other arithmetic, per_device(): return (dq.astype(F32), dk, dv)  2.42 us

profile of v7, /device:TPU:1, one launch (start us, length us, event | category | flops | bytes accessed | tf_op | source)
XLA Modules:
  0.0 91.4 jit_solution(7173848508907957605)
XLA Ops:
  0.6 87.0 %attention_backward.1 = (bf16[64,6144]{1,0:T(8,128)(2,1)}, f32[64,512]{1,0:T(8,128)}, f32[64,512]{1,0:T(8,128)}) custom-call(s32[33]{0:T(128)} %starts_hbm.1, s32[4,33]{1,0:T(4,128)} %bitcast.1, s32[33]{0:T(128)} %lens_hbm.1, bf16[64,6144]{1,0:T(8,128)(2,1)} %q.1, bf16[64,512]{1,0:T(8,128)(2,1)} %k.1, bf16[64,512]{1,0:T(8,128)(2,1)} %v.1, bf16[64,6144]{1,0:T(8,128)(2,1)} %do.1), custom_call_target="tpu_custom_call" | custom-call | tf_op jit(solution)/shard_map/attention_backward/pallas_call | solution.py:635
  87.7 0.0 copy-start.1
  87.7 0.0 copy-start
  87.7 2.4 %convert_element_type.3 = f32[64,6144]{1,0:T(8,128)} convert(bf16[64,6144]{1,0:T(8,128)(2,1)} %get-tuple-element.6) | non-fusion elementwise | flops 393216 | bytes 2359296 | tf_op jit(solution)/shard_map/convert_element_type | solution.py:652
  90.1 0.0 copy-done.1
  90.1 0.7 copy.12
  90.8 0.0 copy-done
  90.8 0.7 copy.13
Async XLA Ops:
  87.7 2.4 %copy-start.1 = (f32[64,512]{1,0:T(8,128)S(1)}, f32[64,512]{1,0:T(8,128)}, u32[]{:S(2)}) copy-start(f32[64,512]{1,0:T(8,128)} %get-tuple-element.13) | copy-start | bytes 393220
  87.7 3.1 %copy-start = (f32[64,512]{1,0:T(8,128)S(1)}, f32[64,512]{1,0:T(8,128)}, u32[]{:S(2)}) copy-start(f32[64,512]{1,0:T(8,128)} %get-tuple-element.14) | copy-start | bytes 393220
